TPU v7x, 32 devices: a whole 2x2x4 slice. The times are simulated.
32 devices in a mesh: seq: 4 (over y, x), dp: 8 (over z, core).
Axes of the slice: x: 2, y: 2, z: 4, core: 2. Of those that a mesh axis runs over, the one named last changes fastest.
Arguments:
- frames: bfloat16 [8, 1024, 1024], P('dp', 'seq'), may hold values from -6 to 6
- segment_ids: int32 [8, 1024], P('dp'), may hold values from 0 to 1, never falling along the last dimension, each value on 1 to 1000 neighbouring positions
- span_starts: int32 [8, 40], P('dp'), may hold values from 0 to 1014
- cotangent: bfloat16 [8, 1024, 1024], P('dp', 'seq'), may hold values from -6 to 6
- attn_master: float32 [1024, 4096], P('seq', 'dp')
- attn_first: float32 [1024, 4096], P('seq', 'dp'), may hold values from -0.00048828125 to 0.00048828125
- attn_second: float32 [1024, 4096], P('seq', 'dp'), may hold values from 3.973643e-11 to 6.3578287e-10
- ffn_master: float32 [4096, 2048], P('seq', 'dp')
- ffn_first: float32 [4096, 2048], P('seq', 'dp'), may hold values from -0.00048828125 to 0.00048828125
- ffn_second: float32 [4096, 2048], P('seq', 'dp'), may hold values from 3.973643e-11 to 6.3578287e-10
- vec_master: float32 [13, 1024], replicated
- vec_first: float32 [13, 1024], replicated, may hold values from -0.00048828125 to 0.00048828125
- vec_second: float32 [13, 1024], replicated, may hold values from 3.973643e-11 to 6.3578287e-10
Outputs:
- output: bfloat16 [8, 1024, 1024], P('dp', 'seq')
- frames_grad: float32 [8, 1024, 1024], P('dp', 'seq')
- grad_norm: float32 [], replicated
- attn_master_new: float32 [1024, 4096], P('seq', 'dp')
- attn_first_new: float32 [1024, 4096], P('seq', 'dp')
- attn_second_new: float32 [1024, 4096], P('seq', 'dp')
- attn_copy: bfloat16 [1024, 4096], P('seq', 'dp')
- ffn_master_new: float32 [4096, 2048], P('seq', 'dp')
- ffn_first_new: float32 [4096, 2048], P('seq', 'dp')
- ffn_second_new: float32 [4096, 2048], P('seq', 'dp')
- ffn_copy: bfloat16 [4096, 2048], P('seq', 'dp')
- vec_master_new: float32 [13, 1024], replicated
- vec_first_new: float32 [13, 1024], replicated
- vec_second_new: float32 [13, 1024], replicated
Inputs may be any that keep to these rules, and one draw needn't show every extreme that they name: `segment_ids`: each group holds 2 utterances one after another, each of 1 to 1000 frames.
All inputs are finite; a program needn't handle non-finite values.
Results may differ from a plain program's by a relative error of at most 0.012.
The roundings to bfloat16 on the way count: a program that leaves them out, or rounds other values in their place, can miss the bound.
Values may be sent and summed in bfloat16 or wider, within the bound.
A program may use at most 128 MiB of HBM per device.

v0:
```python
import jax
import jax.numpy as jnp
from jax import lax
from jax.sharding import PartitionSpec as P

H = 16
SPAN = 10
STEP = 10


EPS_NORM = 1e-05
BETA_ONE = 0.9
BETA_TWO = 0.999
EPS_ADAM = 1e-08
RATE_ATTN = 0.12
RATE_FFN = 0.03
RATE_VEC = 0.5
DECAY_RATE = 0.01
MAX_NORM = 1.0
NEG_FILL = -1e30


def layer_norm(source, gain_row, shift_row):
    mean_val = jnp.mean(source, axis=-1, keepdims=True)
    centred = source - mean_val
    inv_std = lax.rsqrt(jnp.mean(centred * centred, axis=-1, keepdims=True) + EPS_NORM)
    normed = centred * inv_std
    return (normed * gain_row + shift_row, normed, inv_std)


def norm_back(grad_out, normed, inv_std, gain_row):
    scaled = grad_out * gain_row
    inner = (
        scaled
        - jnp.mean(scaled, axis=-1, keepdims=True)
        - normed * jnp.mean(scaled * normed, axis=-1, keepdims=True)
    )
    return (inner * inv_std, jnp.sum(grad_out * normed, axis=0), jnp.sum(grad_out, axis=0))


def cross_rows(left, right):
    return jnp.einsum("ti,tj->ij", left, right, preferred_element_type=jnp.float32)


def adam_step(master, first, second, grad, rate, decay):
    first_new = BETA_ONE * first + (1.0 - BETA_ONE) * grad
    second_new = BETA_TWO * second + (1.0 - BETA_TWO) * grad * grad
    first_hat = first_new / (1.0 - BETA_ONE**STEP)
    second_hat = second_new / (1.0 - BETA_TWO**STEP)
    master_new = master - rate * (first_hat / (jnp.sqrt(second_hat) + EPS_ADAM) + decay * master)
    return (master_new, first_new, second_new)


def lay_out(whole, seq_count):
    total, rows, cols = whole.shape
    dp_count = total // seq_count
    return (
        whole.reshape(seq_count, dp_count, rows, cols)
        .transpose(0, 2, 1, 3)
        .reshape(seq_count * rows, dp_count * cols)
    )


def split_heads(head_block, segment_row, head_count):
    total_rows = head_block.shape[0]
    local_width = head_block.shape[2]
    head_size = local_width // head_count
    block_rows = min(512, total_rows)
    block_count = total_rows // block_rows
    queries = head_block[:, 0, :].reshape(block_count, block_rows, head_count, head_size)
    key_heads = head_block[:, 1, :].reshape(total_rows, head_count, head_size)
    value_heads = head_block[:, 2, :].reshape(total_rows, head_count, head_size)
    query_segs = segment_row.reshape(block_count, block_rows)
    return (queries, key_heads, value_heads, query_segs)


def block_scores(query_block, key_heads, query_seg, segment_row):
    head_size = query_block.shape[-1]
    raw = jnp.einsum(
        "qhd,khd->hqk", query_block, key_heads, preferred_element_type=jnp.float32
    ) * head_size ** (-0.5)
    same_utt = query_seg[None, :, None] == segment_row[None, None, :]
    return jnp.where(same_utt, raw, NEG_FILL)


def attention_forward(head_block, segment_row, head_count):
    total_rows = head_block.shape[0]
    local_width = head_block.shape[2]
    queries, key_heads, value_heads, query_segs = split_heads(head_block, segment_row, head_count)

    def one_block(pieces):
        query_block, query_seg = pieces
        scores = block_scores(query_block, key_heads, query_seg, segment_row)
        row_peak = jnp.max(scores, axis=-1, keepdims=True)
        expo_terms = jnp.exp(scores - row_peak)
        row_total = jnp.sum(expo_terms, axis=-1, keepdims=True)
        prob_low = (expo_terms / row_total).astype(jnp.bfloat16)
        block_out = jnp.einsum(
            "hqk,khd->qhd", prob_low, value_heads, preferred_element_type=jnp.float32
        )
        return (
            block_out.astype(jnp.bfloat16).reshape(query_block.shape[0], local_width),
            (row_peak + jnp.log(row_total))[..., 0],
        )

    mixed_blocks, log_total = lax.map(one_block, (queries, query_segs))
    return (mixed_blocks.reshape(total_rows, local_width), log_total)


def attention_backward(head_block, grad_mixed, log_total, segment_row, head_count):
    total_rows = head_block.shape[0]
    local_width = head_block.shape[2]
    queries, key_heads, value_heads, query_segs = split_heads(head_block, segment_row, head_count)
    head_size = local_width // head_count
    scale_factor = head_size ** (-0.5)
    grad_blocks = grad_mixed.reshape(queries.shape)

    def one_block(carry, pieces):
        key_grad, value_grad = carry
        query_block, grad_block, total_block, query_seg = pieces
        scores = block_scores(query_block, key_heads, query_seg, segment_row)
        probabilities = jnp.exp(scores - total_block[..., None])
        grad_prob = jnp.einsum(
            "qhd,khd->hqk", grad_block, value_heads, preferred_element_type=jnp.float32
        )
        row_delta = jnp.sum(probabilities * grad_prob, axis=-1, keepdims=True)
        grad_score = (probabilities * (grad_prob - row_delta)).astype(jnp.bfloat16)
        query_grad = (
            jnp.einsum("hqk,khd->qhd", grad_score, key_heads, preferred_element_type=jnp.float32)
            * scale_factor
        )
        key_grad = (
            key_grad
            + jnp.einsum(
                "hqk,qhd->khd", grad_score, query_block, preferred_element_type=jnp.float32
            )
            * scale_factor
        )
        value_grad = value_grad + jnp.einsum(
            "hqk,qhd->khd",
            probabilities.astype(jnp.bfloat16),
            grad_block,
            preferred_element_type=jnp.float32,
        )
        return ((key_grad, value_grad), query_grad)

    zero_heads = jnp.zeros((total_rows, head_count, head_size), jnp.float32)
    (key_grad, value_grad), query_grads = lax.scan(
        one_block, (zero_heads, zero_heads), (queries, grad_blocks, log_total, query_segs)
    )
    stacked = jnp.stack(
        [
            query_grads.reshape(total_rows, local_width),
            key_grad.reshape(total_rows, local_width),
            value_grad.reshape(total_rows, local_width),
        ],
        axis=1,
    )
    return stacked.astype(jnp.bfloat16)


def per_device(
    frames,
    segment_ids,
    span_starts,
    cotangent,
    attn_master,
    attn_first,
    attn_second,
    ffn_master,
    ffn_first,
    ffn_second,
    vec_master,
    vec_first,
    vec_second,
):
    model_width = vec_master.shape[1]
    hidden = (vec_master.shape[0] - 9) * model_width
    seq_count = lax.axis_size("seq")
    seq_rank = lax.axis_index("seq")
    local_rows = frames.shape[1]
    head_local = H // seq_count
    attn_parts, ffn_parts = (
        lax.all_gather(attn_master.astype(jnp.bfloat16)[None], ("seq", "dp"), axis=0, tiled=True),
        lax.all_gather(ffn_master.astype(jnp.bfloat16)[None], ("seq", "dp"), axis=0, tiled=True),
    )
    attn_full = lay_out(attn_parts, seq_count)
    ffn_full = lay_out(ffn_parts, seq_count)
    w_qkv = (
        attn_full[:, : 3 * model_width]
        .reshape(model_width, 3, model_width)
        .transpose(2, 1, 0)
        .reshape(model_width, 3 * model_width)
    )
    w_proj = attn_full[:, 3 * model_width :]
    w_inner = ffn_full[:, :model_width].T
    w_outer = ffn_full[:, model_width:]
    positions = seq_rank * local_rows + lax.iota(jnp.int32, local_rows)
    starts = span_starts[0]
    inside = (positions[:, None] >= starts[None, :]) & (positions[:, None] < starts[None, :] + SPAN)
    masked = jnp.any(inside, axis=1)
    x_in = jnp.where(masked[:, None], vec_master[8][None, :], frames[0].astype(jnp.float32))
    segment_row = segment_ids[0]

    def project(x_value):
        a_val, normed, inv_std = layer_norm(x_value, vec_master[0], vec_master[1])
        a_low = a_val.astype(jnp.bfloat16)
        qkv = jnp.dot(a_low, w_qkv, preferred_element_type=jnp.float32)
        qkv_bias = jnp.stack([vec_master[2], jnp.zeros_like(vec_master[2]), vec_master[3]])
        qkv_low = (qkv.reshape(local_rows, 3, model_width) + qkv_bias[None]).astype(jnp.bfloat16)
        return (a_low, normed, inv_std, qkv_low)

    a_low, normed_one, inv_one, qkv_low = project(x_in)
    head_block = lax.all_to_all(qkv_low, "seq", split_axis=2, concat_axis=0, tiled=True)
    mixed, log_total = attention_forward(head_block, segment_row, head_local)
    attended = lax.all_to_all(mixed, "seq", split_axis=0, concat_axis=1, tiled=True)
    resid = x_in + jnp.dot(attended, w_proj, preferred_element_type=jnp.float32) + vec_master[4]
    b_val, normed_two, inv_two = layer_norm(resid, vec_master[5], vec_master[6])
    b_low = b_val.astype(jnp.bfloat16)
    pre_act = jnp.dot(b_low, w_inner, preferred_element_type=jnp.float32) + vec_master[9:].reshape(
        hidden
    )
    act_low = jax.nn.gelu(pre_act, approximate=False).astype(jnp.bfloat16)
    output = (
        resid + jnp.dot(act_low, w_outer, preferred_element_type=jnp.float32) + vec_master[7]
    ).astype(jnp.bfloat16)
    grad_y = cotangent[0]
    grad_out32 = grad_y.astype(jnp.float32)
    grad_act = jnp.einsum("td,fd->tf", grad_y, w_outer, preferred_element_type=jnp.float32)
    gelu_back = jax.vjp(lambda entry: jax.nn.gelu(entry, approximate=False), pre_act)[1]
    grad_pre = gelu_back(grad_act)[0].astype(jnp.bfloat16)
    b_group, cot_group = (
        lax.all_gather(b_low, "seq", axis=0, tiled=True),
        lax.all_gather(grad_y, "seq", axis=0, tiled=True),
    )
    act_cols, pre_cols = (
        lax.all_to_all(act_low, "seq", split_axis=1, concat_axis=0, tiled=True),
        lax.all_to_all(grad_pre, "seq", split_axis=1, concat_axis=0, tiled=True),
    )
    ffn_rows = jnp.concatenate(
        [cross_rows(pre_cols, b_group), cross_rows(act_cols, cot_group)], axis=1
    )
    g_inner_bias = jnp.sum(grad_pre.astype(jnp.float32), axis=0)
    g_outer_bias = jnp.sum(grad_out32, axis=0)
    grad_b = jnp.einsum("tf,df->td", grad_pre, w_inner, preferred_element_type=jnp.float32)
    grad_ln_two, g_gain_two, g_shift_two = norm_back(grad_b, normed_two, inv_two, vec_master[5])
    grad_resid = grad_out32 + grad_ln_two
    grad_attn = grad_resid.astype(jnp.bfloat16)
    g_proj_bias = jnp.sum(grad_attn.astype(jnp.float32), axis=0)
    grad_attended = jnp.einsum(
        "td,ed->te", grad_attn, w_proj, preferred_element_type=jnp.float32
    ).astype(jnp.bfloat16)
    grad_mixed = lax.all_to_all(grad_attended, "seq", split_axis=1, concat_axis=0, tiled=True)
    a_use, normed_use, inv_use, qkv_again = project(x_in)
    heads_use = lax.all_to_all(qkv_again, "seq", split_axis=2, concat_axis=0, tiled=True)
    grad_heads_qkv = attention_backward(heads_use, grad_mixed, log_total, segment_row, head_local)
    grad_tokens = lax.all_to_all(grad_heads_qkv, "seq", split_axis=0, concat_axis=2, tiled=True)
    a_group, attn_grad_group = (
        lax.all_gather(a_use, "seq", axis=0, tiled=True),
        lax.all_gather(grad_attn, "seq", axis=0, tiled=True),
    )
    qkv_rows = jnp.einsum(
        "tcr,td->rcd", grad_heads_qkv, a_group, preferred_element_type=jnp.float32
    )
    local_width = grad_heads_qkv.shape[2]
    attn_rows = jnp.concatenate(
        [qkv_rows.reshape(local_width, 3 * model_width), cross_rows(mixed, attn_grad_group)], axis=1
    )
    grad_qkv = grad_tokens.reshape(local_rows, 3 * model_width)
    g_query_bias = jnp.sum(grad_tokens[:, 0, :].astype(jnp.float32), axis=0)
    g_value_bias = jnp.sum(grad_tokens[:, 2, :].astype(jnp.float32), axis=0)
    grad_a = jnp.einsum("tj,dj->td", grad_qkv, w_qkv, preferred_element_type=jnp.float32)
    grad_ln_one, g_gain_one, g_shift_one = norm_back(grad_a, normed_use, inv_use, vec_master[0])
    grad_x_in = grad_resid + grad_ln_one
    frames_grad = jnp.where(masked[:, None], 0.0, grad_x_in)
    g_mask = jnp.sum(jnp.where(masked[:, None], grad_x_in, 0.0), axis=0)
    attn_owned, ffn_owned = (
        lax.psum_scatter(attn_rows, "dp", scatter_dimension=1, tiled=True),
        lax.psum_scatter(ffn_rows, "dp", scatter_dimension=1, tiled=True),
    )
    vec_local = jnp.concatenate(
        [
            jnp.stack(
                [
                    g_gain_one,
                    g_shift_one,
                    g_query_bias,
                    g_value_bias,
                    g_proj_bias,
                    g_gain_two,
                    g_shift_two,
                    g_outer_bias,
                    g_mask,
                ]
            ),
            g_inner_bias.reshape(-1, model_width),
        ],
        axis=0,
    )
    owned_squares = jnp.sum(attn_owned * attn_owned) + jnp.sum(ffn_owned * ffn_owned)
    vec_grad, total_squares = lax.psum((vec_local, owned_squares), ("seq", "dp"))
    grad_norm = jnp.sqrt(total_squares + jnp.sum(vec_grad * vec_grad))
    clip = jnp.minimum(1.0, MAX_NORM / (grad_norm + 1e-06))
    attn_new, attn_first_new, attn_second_new = adam_step(
        attn_master, attn_first, attn_second, attn_owned * clip, RATE_ATTN, DECAY_RATE
    )
    ffn_new, ffn_first_new, ffn_second_new = adam_step(
        ffn_master, ffn_first, ffn_second, ffn_owned * clip, RATE_FFN, DECAY_RATE
    )
    vec_new, vec_first_new, vec_second_new = adam_step(
        vec_master, vec_first, vec_second, vec_grad * clip, RATE_VEC, 0.0
    )
    return (
        output[None],
        frames_grad[None],
        grad_norm,
        attn_new,
        attn_first_new,
        attn_second_new,
        attn_new.astype(jnp.bfloat16),
        ffn_new,
        ffn_first_new,
        ffn_second_new,
        ffn_new.astype(jnp.bfloat16),
        vec_new,
        vec_first_new,
        vec_second_new,
    )


def solution(mesh):
    return jax.shard_map(
        per_device,
        mesh=mesh,
        in_specs=(
            P("dp", "seq", None),
            P("dp", None),
            P("dp", None),
            P("dp", "seq", None),
            P("seq", "dp"),
            P("seq", "dp"),
            P("seq", "dp"),
            P("seq", "dp"),
            P("seq", "dp"),
            P("seq", "dp"),
            P(),
            P(),
            P(),
        ),
        out_specs=(
            P("dp", "seq", None),
            P("dp", "seq", None),
            P(),
            P("seq", "dp"),
            P("seq", "dp"),
            P("seq", "dp"),
            P("seq", "dp"),
            P("seq", "dp"),
            P("seq", "dp"),
            P("seq", "dp"),
            P("seq", "dp"),
            P(),
            P(),
            P(),
        ),
        check_vma=False,
    )
```

profile of v0, /device:TPU:0, one launch (start us, length us, event | category | flops | bytes accessed | tf_op | source)
XLA Modules:
  0.0 732.6 jit_solution(14026902936966972244)
XLA Ops:
  17.2 74.5 %all-gather.16.cloned.1.call-done = bf16[8192,512]{1,0:T(8,128)(2,1)} async-done(((bf16[256,512]{1,0:T(8,128)(2,1)}), bf16[8192,512]{1,0:T(8,128)(2,1)}) %all-gather.16.cloned.1.call-update) | async-done | bytes 8388624 | tf_op jit(solution)/shard_map/all_gather | solution.py:184
  91.7 11.4 %copy.176 = bf16[4,8,256,512]{3,1,2,0:T(8,128)(2,1)} copy(bf16[4,8,256,512]{3,2,1,0:T(8,128)(2,1)} %bitcast.266) | data formatting | bytes 16777216 | tf_op jit(solution)/shard_map/reshape | solution.py:58
  103.1 12.3 %copy.225 = bf16[128,8,8,512]{3,1,2,0:T(8,128)(2,1)} copy(bf16[128,8,8,512]{3,2,1,0:T(8,128)(2,1)} %bitcast.255) | data formatting | bytes 16777216
  115.4 6.2 slice.85
  121.6 8.7 %copy.177 = bf16[1024,3072]{0,1:T(8,128)(2,1)} copy(bf16[1024,3072]{1,0:T(8,128)(2,1)} %slice.85) | data formatting | bytes 12582912 | tf_op jit(solution)/shard_map/slice | solution.py:190
  130.3 8.7 %copy.178 = bf16[1024,3,1024]{0,2,1:T(8,128)(2,1)} copy(bf16[1024,3,1024]{2,0,1:T(8,128)(2,1)} %bitcast.259) | data formatting | bytes 12582912 | tf_op jit(solution)/shard_map/transpose | solution.py:192
  151.2 43.1 %all-to-all-done = bf16[256,3,1024]{0,1,2:T(4,128)(2,1)S(1)} async-done(((bf16[256,3,1024]{0,1,2:T(4,128)(2,1)}), bf16[256,3,1024]{0,1,2:T(4,128)(2,1)S(1)}, u32[]{:S(2)}, u32[]{:S(2)}) %all-to-all-start) | async-done | bytes 1572896 | tf_op jit(solution)/shard_map/all_to_all | solution.py:214
  200.8 16.5 %while.27 = (s32[]{:T(128)}, bf16[2,512,256]{2,1,0:T(8,128)(2,1)}, f32[2,4,512]{2,1,0:T(4,128)S(1)}, s32[2,512]{1,0:T(2,128)S(1)}, s32[1,1024]{1,0:T(1,128)S(1)}...) while((s32[]{:T(128)}, bf16[2,512,256]{2,1,0:T(8,128)(2,1)}, ...), condition=%wide.region_6.7_spmd, body=%wide.region_3.6_spmd.sunk | while | flops 562690048 | bytes 29960308 | solution.py:106
  222.0 6.3 all-to-all-done.1
  232.4 15.6 %copy.188 = bf16[4,8,1024,256]{3,1,2,0:T(8,128)(2,1)S(1)} copy(bf16[4,8,1024,256]{3,2,1,0:T(8,128)(2,1)} %bitcast.265) | data formatting | bytes 33554432 | tf_op jit(solution)/shard_map/reshape | solution.py:58
  252.2 13.7 %multiply_convert_fusion.1 = (bf16[256,4096]{1,0:T(8,128)(2,1)}, f32[256,4096]{1,0:T(8,128)S(1)}, f32[256,4096]{1,0:T(8,128)}) fusion(f32[4096]{0:T(1024)S(1)} %bitcast.299, bf16[256,1024]{1,0:T(8,128)(2,1)S(1)} %add_convert_fusion.2, bf16[4096,2048]{1,0:T(8,128)(2,1)S(1)} %bitcast.261), kind=kOutput, calls=%fused_computation.67 | convolution fusion | flops 2216689664 | bytes 19415040 | tf_op jit(solution)/shard_map/dot_general | solution.py:220
  266.0 9.0 %convert_reduce_fusion = (f32[4096]{0:T(1024)}, bf16[256,4096]{1,0:T(8,128)(2,1)S(1)}) fusion(f32[256,4096]{1,0:T(8,128)S(1)} %get-tuple-element.403, f32[256,4096]{1,0:T(8,128)} %get-tuple-element.424, bf16[4096,2048]{1,0:T(8,128)(2,1)} %bitcast.262, bf16[1,256,1024]{2,1,0:T(8,128)(2,1)S(1)} %copy-done.26), kind=kOutput, calls=%fused_computation.65 | convolution fusion | flops 2164256768 | bytes 19415040 | tf_op jit(solution)/shard_map/td,fd->tf/dot_general | solution.py:229
  275.0 7.4 %multiply_reduce_fusion.1 = (f32[1024]{0:T(1024)}, f32[256]{0:T(256)S(1)}, f32[256]{0:T(256)S(1)}, f32[1024]{0:T(1024)}, f32[256,1024]{1,0:T(8,128)S(1)}) fusion(f32[256,1024]{1,0:T(8,128)S(1)} %get-tuple-element.423, f32[256]{0:T(256)S(1)} %add_rsqrt_fusion, f32[256]{0:T(256)S(1)} %broadcast_multiply_fusion.4, f32[1024]{0:T(1024)S(1)} %bitcast.294, ...), kind=kOutput, calls=%fused_computation.131 | convolution fusion | flops 2149840384 | bytes 12599296 | tf_op jit(solution)/shard_map/tf,df->td/dot_general | solution.py:245
  302.1 39.4 %while.28 = (s32[]{:T(128)}, f32[1024,4,64]{0,2,1:T(8,128)S(1)}, f32[1024,4,64]{0,2,1:T(8,128)}, bf16[2,512,4,64]{1,3,2,0:T(8,128)(2,1)}, bf16[2,512,4,64]{1,3,2...) while((s32[]{:T(128)}, f32[1024,4,64]{0,2,1:T(8,128)S(1)}, ...), condition=%wide.region_13.14_spmd.clone, body=%wide.region_11.13_spmd.clone.sunk | while | flops 1375598592 | bytes 164694384 | solution.py:148
  346.5 25.2 %all_to_all.114 = bf16[1024,3,256]{2,1,0:T(4,128)(2,1)S(1)} all-to-all(bf16[1024,3,256]{2,1,0:T(4,128)(2,1)S(1)} %copy.197), channel_id=1, replica_groups=mesh['seq'=4,'dp'=8] {'seq'}, dimensions={0} | all-to-all | bytes 3145728 | tf_op jit(solution)/shard_map/all_to_all | solution.py:257
  373.6 6.5 fusion.107
  384.9 28.0 %all-gather.10.cloned.1.call-done = bf16[1024,1024]{1,0:T(8,128)(2,1)} async-done(((bf16[256,1024]{1,0:T(8,128)(2,1)}), bf16[1024,1024]{1,0:T(8,128)(2,1)}) %all-gather.10.cloned.1.call-update) | async-done | bytes 2097168 | tf_op jit(solution)/shard_map/all_gather | solution.py:259
  433.3 34.9 %all-to-all-done.5 = bf16[256,4,1024]{2,0,1:T(8,128)(2,1)} async-done(((bf16[256,4,1024]{2,0,1:T(8,128)(2,1)}), bf16[256,4,1024]{2,0,1:T(8,128)(2,1)}, u32[]{:S(2)}, u32[]{:S(2)}) %all-to-all-start.5) | async-done | bytes 2097184 | tf_op jit(solution)/shard_map/all_to_all | solution.py:237
  472.1 6.5 fusion.61
  478.6 42.1 %all-gather.14.cloned.1.call-done = bf16[1024,1024]{1,0:T(8,128)(2,1)} async-done(((bf16[256,1024]{1,0:T(8,128)(2,1)}), bf16[1024,1024]{1,0:T(8,128)(2,1)}) %all-gather.14.cloned.1.call-update) | async-done | bytes 2097168 | tf_op jit(solution)/shard_map/all_gather | solution.py:233
  534.7 7.4 %fusion.89 = bf16[1,256,1024]{2,1,0:T(8,128)(2,1)} fusion(f32[256,1024]{1,0:T(8,128)S(1)} %copy-done.5, bf16[256,4096]{1,0:T(8,128)(2,1)} %get-tuple-element.402, bf16[4096,2048]{1,0:T(8,128)(2,1)} %bitcast.264, f32[1024]{0:T(1024)S(1)} %bitcast.306), kind=kOutput, calls=%fused_computation.104 | convolution fusion | flops 2148270080 | bytes 12062720 | tf_op jit(solution)/shard_map/dot_general | solution.py:225
  544.2 28.9 %reduce-scatter.3.cloned.1.call-done = f32[256,512]{1,0:T(8,128)} async-done(((f32[256,4096]{1,0:T(8,128)}), f32[256,512]{1,0:T(8,128)}) %reduce-scatter.3.cloned.1.call-update) | async-done | bytes 524304 | tf_op jit(solution)/shard_map/reduce_scatter | solution.py:278
  574.8 88.3 %reduce-scatter.5.cloned.1.call-done = f32[1024,256]{0,1:T(8,128)} async-done(((f32[1024,2048]{0,1:T(8,128)}), f32[1024,256]{0,1:T(8,128)}) %reduce-scatter.5.cloned.1.call-update) | async-done | bytes 1048592 | tf_op jit(solution)/shard_map/reduce_scatter | solution.py:279
  668.9 38.7 %all-reduce = (f32[]{:T(128)}, f32[13,1024]{1,0:T(8,128)S(1)}) all-reduce(f32[]{:T(128)S(6)} %add.234, f32[13,1024]{1,0:T(8,128)S(1)} %concatenate.11), channel_id=1, replica_groups=mesh['seq'=4,'dp'=8] {'seq','dp'}, use_global_device_ids=true, to_apply=%region_20.21 | all-reduce | flops 13313 | bytes 106504 | tf_op jit(solution)/shard_map/psum | solution.py:301
  (267 shorter events, 189.6 us)
Async XLA Ops:
  7.2 84.5 %all-gather.16.cloned.1.call-start = ((), (), s32[]{:S(2)}) async-start(), calls=%async_computation.13 | async-start | bytes 8650752 | tf_op jit(solution)/shard_map/all_gather | solution.py:184
  9.0 223.4 %all-gather.18.cloned.1.call-start = ((), (), s32[]{:S(2)}) async-start(), calls=%async_computation.14 | async-start | bytes 17301504 | tf_op jit(solution)/shard_map/all_gather | solution.py:185
  12.7 216.5 %copy-start.44 = (pred[256]{0:T(512)(128)(4,1)}, pred[256]{0:T(512)(128)(4,1)S(1)}, u32[]{:S(2)}) copy-start(pred[256]{0:T(512)(128)(4,1)S(1)} %and_reduce_fusion) | copy-start | bytes 772
  14.4 124.6 %copy-start.40 = (f32[1,1024]{1,0:T(1,128)}, f32[1,1024]{1,0:T(1,128)S(1)}, u32[]{:S(2)}) copy-start(f32[1,1024]{1,0:T(1,128)S(1)} %get-tuple-element.420) | copy-start | bytes 12292
  14.4 124.6 %copy-start.49 = (f32[1,1024]{1,0:T(1,128)}, f32[1,1024]{1,0:T(1,128)S(1)}, u32[]{:S(2)}) copy-start(f32[1,1024]{1,0:T(1,128)S(1)} %get-tuple-element.419) | copy-start | bytes 12292
  14.4 214.8 %copy-start.37 = (f32[1,1024]{1,0:T(1,128)}, f32[1,1024]{1,0:T(1,128)S(1)}, u32[]{:S(2)}) copy-start(f32[1,1024]{1,0:T(1,128)S(1)} %get-tuple-element.421) | copy-start | bytes 12292
  15.7 123.2 %copy-start.46 = (f32[256]{0:T(256)}, f32[256]{0:T(256)S(1)}, u32[]{:S(2)}) copy-start(f32[256]{0:T(256)S(1)} %broadcast_multiply_fusion.5) | copy-start | bytes 3076
  17.1 121.9 %copy-start.53 = (f32[256]{0:T(256)}, f32[256]{0:T(256)S(1)}, u32[]{:S(2)}) copy-start(f32[256]{0:T(256)S(1)} %add_rsqrt_fusion.1) | copy-start | bytes 3076
  146.4 47.9 %all-to-all-start = ((bf16[256,3,1024]{0,1,2:T(4,128)(2,1)}), bf16[256,3,1024]{0,1,2:T(4,128)(2,1)S(1)}, u32[]{:S(2)}, u32[]{:S(2)}) async-start(bf16[256,3,1024]{0,1,2:T(4,128)(2,1)} %copy.179), calls=%async_computation | async-start | bytes 4194304 | tf_op jit(solution)/shard_map/all_to_all | solution.py:214
  217.3 10.9 %all-to-all-start.1 = ((bf16[4,256,256]{2,1,0:T(8,128)(2,1)}), bf16[4,256,256]{2,1,0:T(8,128)(2,1)S(1)}, u32[]{:S(2)}, u32[]{:S(2)}) async-start(bf16[4,256,256]{2,1,0:T(8,128)(2,1)} %bitcast.26), calls=%async_computation.1 | async-start | bytes 1048576 | tf_op jit(solution)/shard_map/all_to_all | solution.py:216
  231.8 50.6 %copy-start.4 = (f32[256,1024]{1,0:T(8,128)}, f32[256,1024]{1,0:T(8,128)S(1)}, u32[]{:S(2)}) copy-start(f32[256,1024]{1,0:T(8,128)S(1)} %get-tuple-element.423) | copy-start | bytes 3145732
  232.4 19.9 %copy-start.23 = (bf16[256,1024]{1,0:T(8,128)(2,1)}, bf16[256,1024]{1,0:T(8,128)(2,1)S(1)}, u32[]{:S(2)}) copy-start(bf16[256,1024]{1,0:T(8,128)(2,1)S(1)} %add_convert_fusion.2) | copy-start | bytes 1572868
  252.2 13.8 %copy-start.3 = (bf16[512,8,8,256]{3,1,2,0:T(8,128)(2,1)}, bf16[512,8,8,256]{3,1,2,0:T(8,128)(2,1)S(1)}, u32[]{:S(2)}) copy-start(bf16[512,8,8,256]{3,1,2,0:T(8,128)(2,1)S(1)} %copy.226) | copy-start | bytes 50331652
  288.1 10.0 %all-to-all-start.2 = ((bf16[256,4,256]{0,2,1:T(8,128)(2,1)}), bf16[256,4,256]{0,2,1:T(8,128)(2,1)S(1)}, u32[]{:S(2)}, u32[]{:S(2)}) async-start(bf16[256,4,256]{0,2,1:T(8,128)(2,1)} %bitcast.37), calls=%async_computation.2 | async-start | bytes 1048576 | tf_op jit(solution)/shard_map/all_to_all | solution.py:253
  291.6 89.8 %all-gather.12.cloned.1.call-start = ((), (), s32[]{:S(2)}) async-start(), calls=%async_computation.9 | async-start | bytes 2621440 | tf_op jit(solution)/shard_map/all_gather | solution.py:260
  292.3 120.6 %all-gather.10.cloned.1.call-start = ((), (), s32[]{:S(2)}) async-start(), calls=%async_computation.8 | async-start | bytes 2621440 | tf_op jit(solution)/shard_map/all_gather | solution.py:259
  380.1 32.8 %copy-start.25 = (bf16[1024,1,256]{2,0,1:T(8,128)(2,1)S(1)}, bf16[1024,1,256]{2,0,1:T(8,128)(2,1)}, u32[]{:S(2)}) copy-start(bf16[1024,1,256]{2,0,1:T(8,128)(2,1)} %copy-done.24) | copy-start | bytes 1572868
  380.2 91.9 %all-gather.20.cloned.1.call-start = ((), (), s32[]{:S(2)}) async-start(), calls=%async_computation.15 | async-start | bytes 2621440 | tf_op jit(solution)/shard_map/all_gather | solution.py:234
  380.8 140.0 %all-gather.14.cloned.1.call-start = ((), (), s32[]{:S(2)}) async-start(), calls=%async_computation.11 | async-start | bytes 2621440 | tf_op jit(solution)/shard_map/all_gather | solution.py:233
  381.3 191.7 %reduce-scatter.3.cloned.1.call-start = ((), (), s32[]{:S(2)}) async-start(), calls=%async_computation.10 | async-start | bytes 4718592 | tf_op jit(solution)/shard_map/reduce_scatter | solution.py:278
  427.1 41.0 %all-to-all-start.5 = ((bf16[256,4,1024]{2,0,1:T(8,128)(2,1)}), bf16[256,4,1024]{2,0,1:T(8,128)(2,1)}, u32[]{:S(2)}, u32[]{:S(2)}) async-start(bf16[256,4,1024]{2,0,1:T(8,128)(2,1)} %bitcast.206), calls=%async_computation.6 | async-start | bytes 4194304 | tf_op jit(solution)/shard_map/all_to_all | solution.py:237
  468.2 52.6 %all-to-all-start.4 = ((bf16[256,4,1024]{2,0,1:T(8,128)(2,1)}), bf16[256,4,1024]{2,0,1:T(8,128)(2,1)S(1)}, u32[]{:S(2)}, u32[]{:S(2)}) async-start(bf16[256,4,1024]{2,0,1:T(8,128)(2,1)} %bitcast.207), calls=%async_computation.5 | async-start | bytes 4194304 | tf_op jit(solution)/shard_map/all_to_all | solution.py:238
  471.8 191.4 %reduce-scatter.5.cloned.1.call-start = ((), (), s32[]{:S(2)}) async-start(), calls=%async_computation.12 | async-start | bytes 9437184 | tf_op jit(solution)/shard_map/reduce_scatter | solution.py:279
  542.2 167.4 %copy-start.12 = (f32[1024,256]{0,1:T(8,128)S(1)}, f32[1024,256]{0,1:T(8,128)}, u32[]{:S(2)}) copy-start(f32[1024,256]{0,1:T(8,128)} %copy.207) | copy-start | bytes 3145732
  (51 other events, 228.7 us)
Sparse Core Ops, SparseCore 0:
  11.6 80.0 all-gather.15
  95.3 131.4 all-gather.17
  294.9 35.2 all-gather.11
  380.3 32.5 all-gather.9
  414.6 53.6 all-gather.19
  470.6 50.0 all-gather.13
  523.0 50.0 reduce-scatter.2
  575.4 87.7 reduce-scatter.4
where the time goes:
time: 744 us; the launch traced here: 733 us
  waiting for transfers between devices  353 us (47%)
  local copies, waits for them, and re-layouts  117 us (16%)
  matrix products  109 us (15%)
  blocking collectives  63.9 us (9%)
  other arithmetic  49.7 us (7%)
  starting transfers between devices  20 us (3%)
  between operations  19.2 us (3%)
    reduce_scatter x1, waiting for transfers between devices, per_device(): lax.psum_scatter(ffn_rows, 'dp', scatter_dimension=1, tiled=True)  88.3 us
    all_gather x1, waiting for transfers between devices, per_device(): lax.all_gather(attn_master.astype(jnp.bfloat16)[None], ('seq', 'dp'), axi...  74.5 us
    all_to_all x1, waiting for transfers between devices, per_device(): lax.all_to_all(qkv_low, 'seq', split_axis=2, concat_axis=0, tiled=True)  43.1 us
    all_gather x1, waiting for transfers between devices, per_device(): lax.all_gather(b_low, 'seq', axis=0, tiled=True)  42.1 us
    psum x1, blocking collectives, per_device(): lax.psum((vec_local, owned_squares), ('seq', 'dp'))  38.7 us
    all_to_all x1, waiting for transfers between devices, per_device(): lax.all_to_all(act_low, 'seq', split_axis=1, concat_axis=0, tiled=True)  34.9 us
    unnamed x109, local copies, waits for them, and re-layouts  33.5 us
    reduce_scatter x1, waiting for transfers between devices, per_device(): lax.psum_scatter(attn_rows, 'dp', scatter_dimension=1, tiled=True)  28.9 us
  transfers between devices with their start and end apart: 13, of which 9 were waited for; matrix products, arithmetic and copies ran while one was open for 26% of the time, Pallas kernels for 0%

commit v1 on v0

v1 whole, which is shorter than its diff:
```python
import functools

import jax
import jax.numpy as jnp
from jax import lax
from jax.experimental import pallas as pl
from jax.experimental.pallas import tpu as pltpu
from jax.sharding import PartitionSpec as P

H = 16
SPAN = 10
STEP = 10

EPS_NORM = 1e-05
BETA_ONE = 0.9
BETA_TWO = 0.999
EPS_ADAM = 1e-08
RATE_ATTN = 0.12
RATE_FFN = 0.03
RATE_VEC = 0.5
DECAY_RATE = 0.01
MAX_NORM = 1.0
NEG_FILL = -1e30

SLABS = 8
LANES = 128
F32 = jnp.float32
BF16 = jnp.bfloat16
MESH = pl.DeviceIdType.MESH


def adam_step(master, first, second, grad, rate, decay):
    first_new = BETA_ONE * first + (1.0 - BETA_ONE) * grad
    second_new = BETA_TWO * second + (1.0 - BETA_TWO) * grad * grad
    first_hat = first_new / (1.0 - BETA_ONE**STEP)
    second_hat = second_new / (1.0 - BETA_TWO**STEP)
    master_new = master - rate * (first_hat / (jnp.sqrt(second_hat) + EPS_ADAM) + decay * master)
    return (master_new, first_new, second_new)


def nn(left, right):
    return lax.dot_general(left, right, (((1,), (0,)), ((), ())), preferred_element_type=F32)


def nt(left, right):
    return lax.dot_general(left, right, (((1,), (1,)), ((), ())), preferred_element_type=F32)


def tn(left, right):
    return lax.dot_general(left, right, (((0,), (0,)), ((), ())), preferred_element_type=F32)


def normalise(source):
    mean_val = jnp.mean(source, axis=-1, keepdims=True)
    centred = source - mean_val
    inv_std = lax.rsqrt(jnp.mean(centred * centred, axis=-1, keepdims=True) + EPS_NORM)
    return centred * inv_std, inv_std


def norm_back(grad_out, normed, inv_std, gain_row):
    scaled = grad_out * gain_row
    inner = (
        scaled
        - jnp.mean(scaled, axis=-1, keepdims=True)
        - normed * jnp.mean(scaled * normed, axis=-1, keepdims=True)
    )
    return inner * inv_std


def col_sum(value):
    return jnp.sum(value, axis=0, keepdims=True)


class Gather:
    def __init__(self, cp, buf, base, place, off, rows):
        self.cp, self.buf, self.b = cp, buf, base
        self.s, self.px, self.py, self.pd = place
        self.off, self.h = off, rows // 2

    def top(self, slot):
        return self.buf.at[slot, pl.ds(self.off, self.h)]

    def bot(self, slot):
        return self.buf.at[slot, pl.ds(self.off + self.h, self.h)]

    def c(self, part, slot, i, to):
        ref = part(slot)
        return self.cp(ref, ref, self.b + i, to)

    def start(self):
        self.c(self.top, self.s, 0, self.px).start()
        self.c(self.bot, self.s, 2, self.py).start()
        self.c(self.bot, self.s, 1, self.px).start()
        self.c(self.top, self.s, 3, self.py).start()

    def relay(self):
        self.c(self.top, self.px, 0, self.px).wait_recv()
        self.c(self.top, self.px, 4, self.py).start()
        self.c(self.bot, self.py, 2, self.py).wait_recv()
        self.c(self.bot, self.py, 5, self.px).start()

    def wait_x(self):
        self.c(self.bot, self.px, 1, self.px).wait_recv()

    def wait_y(self):
        self.c(self.top, self.py, 3, self.py).wait_recv()

    def wait_d(self):
        self.c(self.top, self.pd, 4, self.py).wait_recv()
        self.c(self.bot, self.pd, 5, self.px).wait_recv()

    def sent(self):
        for part, slot, i, to in (
            (self.top, self.s, 0, self.px),
            (self.bot, self.s, 2, self.py),
            (self.bot, self.s, 1, self.px),
            (self.top, self.s, 3, self.py),
            (self.top, self.px, 4, self.py),
            (self.bot, self.py, 5, self.px),
        ):
            self.c(part, slot, i, to).wait_send()


class Scatter:
    def __init__(self, cp, part, in_x, in_y, via_x, via_y, base, place):
        _, px, py, _ = place
        h = in_x.shape[0] // 2
        top, bot = pl.ds(0, h), pl.ds(h, h)
        self.part, self.via_x, self.via_y, self.h = part, via_x, via_y, h
        self.copies = [
            cp(part.at[2, top], via_x, base, px),
            cp(part.at[2, bot], via_y, base + 1, py),
            cp(part.at[0, top], in_x.at[top], base + 2, px),
            cp(part.at[1, bot], in_y.at[bot], base + 3, py),
            cp(part.at[1, top], in_y.at[top], base + 4, py),
            cp(part.at[0, bot], in_x.at[bot], base + 5, px),
        ]

    def start(self, relation):
        for i in {3: (0, 1), 1: (2,), 2: (3,)}[relation]:
            self.copies[i].start()

    def relay_y(self):
        self.copies[0].wait_recv()
        self.part[1, : self.h, :] = (self.part[1, : self.h, :].astype(F32) + self.via_x[...].astype(F32)).astype(BF16)
        self.copies[4].start()

    def relay_x(self):
        self.copies[1].wait_recv()
        self.part[0, self.h :, :] = (self.part[0, self.h :, :].astype(F32) + self.via_y[...].astype(F32)).astype(BF16)
        self.copies[5].start()

    def wait(self):
        for i in (2, 3, 4, 5):
            self.copies[i].wait_recv()

    def sent(self):
        for copy in self.copies:
            copy.wait_send()


def layer_kernel(
    frames,
    mask_col,
    cot,
    seg_q,
    seg_k,
    vec,
    w_attn,
    w_ffn,
    out,
    frames_grad,
    vec_grad,
    g_attn,
    g_ffn,
    fr_g,
    cot_g,
    a_g,
    wp,
    qa,
    ka,
    va,
    kt,
    att,
    b_g,
    act_g,
    gp_g,
    resid,
    own,
    part,
    part2,
    in_x,
    in_y,
    via_x,
    via_y,
    in_x2,
    in_y2,
    via_x2,
    via_y2,
    gsend,
    gm,
    dom,
    ga_g,
    gres,
    dqkv,
    dk_acc,
    dv_acc,
    send_sem,
    recv_sem,
):
    s = lax.axis_index("seq")
    d = lax.axis_index("dp")
    core = lax.rem(d, 2)
    sib = d + 1 - 2 * core

    def peer(r):
        high = lax.rem(s // 2 + r // 2, 2)
        low = lax.rem(lax.rem(s, 2) + r % 2, 2)
        return 2 * high + low

    px, py, pd = peer(1), peer(2), peer(3)
    place = (s, px, py, pd)

    def cp(src, dst, i, to):
        return pltpu.make_async_remote_copy(
            src_ref=src,
            dst_ref=dst,
            send_sem=send_sem.at[i],
            recv_sem=recv_sem.at[i],
            device_id=(to, d),
            device_id_type=MESH,
        )

    def cp_sib(src, dst, i):
        return pltpu.make_async_remote_copy(
            src_ref=src,
            dst_ref=dst,
            send_sem=send_sem.at[i],
            recv_sem=recv_sem.at[i],
            device_id=(s, sib),
            device_id_type=MESH,
        )

    rows = frames.shape[0]
    width = frames.shape[1]
    local = width // 4
    slab_a = w_attn.shape[2]
    slab_f = w_ffn.shape[2]
    per_a = width // slab_a
    per_f = width // slab_f
    tile = 256
    chunk = 32

    barrier = pltpu.get_barrier_semaphore()
    for to in (px, py, pd):
        pl.semaphore_signal(barrier, inc=1, device_id=(to, d), device_id_type=MESH)
    pl.semaphore_signal(barrier, inc=1, device_id=(s, sib), device_id_type=MESH)
    pl.semaphore_wait(barrier, 4)

    fr_g[s] = frames[...]
    frames_in = Gather(cp, fr_g, 0, place, 0, rows)
    frames_in.start()

    cot_g[s] = cot[...]
    cot_in = Gather(cp, cot_g, 15, place, 0, rows)
    for i in range(per_a):
        wp[s, :, i * slab_a : (i + 1) * slab_a] = w_attn[3 * per_a + i]
    half = rows // 2
    wp_off = pl.multiple_of(core * half, half)
    wp_in = Gather(cp, wp, 6, place, wp_off, half)
    wp_cross = [
        cp_sib(wp.at[p, pl.ds(wp_off, half)], wp.at[p, pl.ds(wp_off, half)], 12 + i) for i, p in enumerate((px, py, pd))
    ]
    vec_grad[...] = jnp.zeros_like(vec_grad)

    lane = lax.broadcasted_iota(jnp.int32, (rows, LANES), 1)
    low_head = lane < LANES // 2
    q_bias = vec[2:3, pl.ds(pl.multiple_of(s * local, local), local)]
    v_bias = vec[3:4, pl.ds(pl.multiple_of(s * local, local), local)]

    def weight_rows(first, count, start, size):
        return jnp.concatenate([w_attn[first + i, start : start + size, :] for i in range(count)], axis=1)

    def enter(blk):
        def norm_rows(i, carry):
            at = pl.ds(pl.multiple_of(i * chunk, chunk), chunk)
            at_all = pl.ds(pl.multiple_of(blk * rows + i * chunk, chunk), chunk)
            x = jnp.where(mask_col[at_all, :] > 0.0, vec[8:9, :], fr_g[blk, at, :].astype(F32))
            normed, _ = normalise(x)
            a_g[blk, at, :] = (normed * vec[0:1, :] + vec[1:2, :]).astype(BF16)
            return carry

        lax.fori_loop(0, rows // chunk, norm_rows, 0)
        a = a_g[blk]
        at_all = pl.ds(pl.multiple_of(blk * rows, rows), rows)
        q = (nt(a, weight_rows(0, per_a, 0, local)) + q_bias).astype(BF16).astype(F32) * 0.125
        for pair in range(2):
            both = q[:, pair * LANES : (pair + 1) * LANES]
            for h in range(2):
                keep = low_head if h == 0 else jnp.logical_not(low_head)
                qa[2 * pair + h, blk, :, :LANES] = jnp.where(keep, both, 0.0).astype(BF16)
                qa[2 * pair + h, blk, :, LANES:] = seg_q[at_all, :]
        k = nt(a, weight_rows(per_a, per_a, 0, local)).astype(BF16)
        for pair in range(2):
            both = k[:, pair * LANES : (pair + 1) * LANES]
            ka[pair, at_all, :LANES] = both
            ka[pair, at_all, LANES:] = seg_k[at_all, :]
            kt[pair, :, at_all] = jnp.transpose(both)
        v = (nt(a, weight_rows(2 * per_a, per_a, 0, local)) + v_bias).astype(BF16)
        for pair in range(2):
            va[pair, at_all, :] = v[:, pair * LANES : (pair + 1) * LANES]

    enter(s)
    frames_in.relay()
    wp_in.start()
    frames_in.wait_x()
    enter(px)
    frames_in.wait_y()
    enter(py)
    frames_in.wait_d()
    enter(pd)
    wp_in.relay()
    cot_in.start()

    def att_x(j, slot):
        return cp(att.at[slot, j], att.at[slot, j], 21 + j, px)

    def att_y(j, slot):
        return cp(att.at[slot, j], att.at[slot, j], 25 + j, py)

    def att_relay(j, start):
        even = lax.rem(j, 2) == 0

        @pl.when(even)
        def _():
            if start:
                att_x(j, px).wait_recv()
                cp(att.at[px, j], att.at[px, j], 29 + j, py).start()
            else:
                cp(att.at[px, j], att.at[px, j], 29 + j, py).wait_send()

        @pl.when(jnp.logical_not(even))
        def _():
            if start:
                att_y(j, py).wait_recv()
                cp(att.at[py, j], att.at[py, j], 29 + j, px).start()
            else:
                cp(att.at[py, j], att.at[py, j], 29 + j, px).wait_send()

    def attend(j, carry):
        for pair in range(2):
            outs = []
            for h in range(2):
                head = 2 * pair + h
                scores = nt(qa[head, j], ka[pair])
                peak = jnp.max(scores, axis=-1, keepdims=True)
                terms = jnp.exp(scores - peak)
                total = jnp.sum(terms, axis=-1, keepdims=True)
                probs = (terms * (1.0 / total)).astype(BF16)
                outs.append(nn(probs, va[pair]))
                log_total = -(peak + jnp.log(total))
                part_one = log_total.astype(BF16).astype(F32)
                rest = log_total - part_one
                part_two = rest.astype(BF16).astype(F32)
                part_three = rest - part_two
                aug = qa[head, j, :, LANES:].astype(F32)
                aug = jnp.where(lane == 2, part_one, aug)
                aug = jnp.where(lane == 3, part_two, aug)
                aug = jnp.where(lane == 4, part_three, aug)
                qa[head, j, :, LANES:] = aug.astype(BF16)
            att[s, j, :, pair * LANES : (pair + 1) * LANES] = jnp.where(low_head, outs[0], outs[1]).astype(BF16)
        att_x(j, s).start()
        att_y(j, s).start()

        @pl.when(j > 0)
        def _():
            att_relay(j - 1, True)

        return carry

    lax.fori_loop(0, 4, attend, 0)
    att_relay(3, True)
    wp_in.wait_x()
    wp_cross[0].start()
    wp_in.wait_y()
    wp_cross[1].start()
    wp_in.wait_d()
    wp_cross[2].start()
    cot_in.relay()
    other_off = pl.multiple_of((1 - core) * half, half)
    for i, p in enumerate((px, py, pd)):
        cp_sib(wp.at[p, pl.ds(other_off, half)], wp.at[p, pl.ds(other_off, half)], 12 + i).wait_recv()

    def project(j, carry):
        even = lax.rem(j, 2) == 0

        @pl.when(even)
        def _():
            att_y(j, py).wait_recv()
            cp(att.at[pd, j], att.at[pd, j], 29 + j, py).wait_recv()

        @pl.when(jnp.logical_not(even))
        def _():
            att_x(j, px).wait_recv()
            cp(att.at[pd, j], att.at[pd, j], 29 + j, px).wait_recv()

        left = jnp.concatenate([att[p, j] for p in range(4)], axis=1)
        for i in range(width // tile):
            right = jnp.concatenate([wp[p, :, i * tile : (i + 1) * tile] for p in range(4)], axis=0)
            own[:, i * tile : (i + 1) * tile] = nn(left, right)

        def norm_rows(i, inner):
            at = pl.ds(pl.multiple_of(i * chunk, chunk), chunk)
            at_all = pl.ds(pl.multiple_of(j * rows + i * chunk, chunk), chunk)
            x = jnp.where(mask_col[at_all, :] > 0.0, vec[8:9, :], fr_g[j, at, :].astype(F32))
            total = x + own[at, :] + vec[4:5, :]

            @pl.when(j == s)
            def _():
                resid[at, :] = total

            normed, _ = normalise(total)
            b_g[j, at, :] = (normed * vec[5:6, :] + vec[6:7, :]).astype(BF16)
            return inner

        lax.fori_loop(0, rows // chunk, norm_rows, 0)
        return carry

    lax.fori_loop(0, 4, project, 0)

    def feed(r):
        blk = peer(r)

        def hidden_tile(i, carry):
            at = pl.ds(pl.multiple_of(i * tile, tile), tile)
            w_in = jnp.concatenate([w_ffn[k, at, :] for k in range(per_f)], axis=1)
            w_out = jnp.concatenate([w_ffn[per_f + k, at, :] for k in range(per_f)], axis=1)
            pre = nt(b_g[blk], w_in) + vec[pl.ds(9 + s, 1), at]
            grad_act = nt(cot_g[blk], w_out)
            cdf = 0.5 * (1.0 + lax.erf(pre * 0.7071067811865476))
            act_g[blk, :, at] = (pre * cdf).astype(BF16)
            density = jnp.exp(-0.5 * pre * pre) * 0.3989422804014327
            grad_pre = ((cdf + pre * density) * grad_act).astype(BF16)
            gp_g[blk, :, at] = grad_pre
            vec_grad[pl.ds(9 + s, 1), at] += col_sum(grad_pre.astype(F32))
            return carry

        lax.fori_loop(0, w_ffn.shape[1] // tile, hidden_tile, 0)
        left = gp_g[blk]
        for k in range(per_f):
            at = slice(k * slab_f, (k + 1) * slab_f)
            value = nn(left, w_ffn[k])
            if r == 0:
                own[:, at] = value
            else:
                part[r - 1, :, at] = value.astype(BF16)

    sum_b = Scatter(cp, part, in_x, in_y, via_x, via_y, 33, place)
    cot_in.wait_x()
    cot_in.wait_y()
    cot_in.wait_d()
    feed(3)
    sum_b.start(3)
    feed(1)
    sum_b.start(1)
    feed(2)
    sum_b.start(2)
    sum_b.relay_y()
    sum_b.relay_x()
    feed(0)
    sum_b.wait()

    def back_two(i, carry):
        at = pl.ds(pl.multiple_of(i * chunk, chunk), chunk)
        grad_b = own[at, :] + in_x[at, :].astype(F32) + in_y[at, :].astype(F32)
        normed, inv_std = normalise(resid[at, :])
        grad_y = cot[at, :].astype(F32)
        grad_resid = grad_y + norm_back(grad_b, normed, inv_std, vec[5:6, :])
        gres[at, :] = grad_resid
        low = grad_resid.astype(BF16)
        ga_g[s, at, :] = low
        vec_grad[4:5, :] += col_sum(low.astype(F32))
        vec_grad[5:6, :] += col_sum(grad_b * normed)
        vec_grad[6:7, :] += col_sum(grad_b)
        vec_grad[7:8, :] += col_sum(grad_y)
        return carry

    lax.fori_loop(0, rows // chunk, back_two, 0)

    for i, r in enumerate((3, 1, 2)):
        gsend[r] = nt(ga_g[s], wp[peer(r)]).astype(BF16)
        cp(gsend.at[r], gm.at[s], 39 + i, peer(r)).start()
    gm[s] = nt(ga_g[s], wp[s]).astype(BF16)
    ga_in = Gather(cp, ga_g, 42, place, 0, rows)
    ga_in.start()
    sum_b.sent()

    sum_o = Scatter(cp, part, in_x2, in_y2, via_x2, via_y2, 48, place)

    def out_part(blk, k):
        return nn(act_g[blk], w_ffn[per_f + k])

    for r in (3, 1, 2):
        for k in range(per_f):
            part[r - 1, :, k * slab_f : (k + 1) * slab_f] = out_part(peer(r), k).astype(BF16)
        sum_o.start(r)

    def ffn_grads(i, carry):
        at = pl.ds(pl.multiple_of(i * tile, tile), tile)
        for left, right, first in ((gp_g, b_g, 0), (act_g, cot_g, per_f)):
            turned = jnp.transpose(jnp.concatenate([left[p, :, at] for p in range(4)], axis=0))
            for k in range(per_f):
                cols = jnp.concatenate([right[p, :, k * slab_f : (k + 1) * slab_f] for p in range(4)], axis=0)
                g_ffn[first + k, at, :] = nn(turned, cols).astype(BF16)
        return carry

    lax.fori_loop(0, w_ffn.shape[1] // tile, ffn_grads, 0)

    for i, r in enumerate((3, 1, 2)):
        cp(gsend.at[r], gm.at[peer(r)], 39 + i, peer(r)).wait_recv()

    def spread(j, carry):
        for pair in range(2):
            both = gm[j, :, pair * LANES : (pair + 1) * LANES].astype(F32)
            dom[2 * pair, j] = jnp.where(low_head, both, 0.0).astype(BF16)
            dom[2 * pair + 1, j] = jnp.where(low_head, 0.0, both).astype(BF16)
        return carry

    lax.fori_loop(0, 4, spread, 0)
    ga_in.relay()
    sum_o.relay_y()
    sum_o.relay_x()

    def back_pair(pair):
        dk_acc[...] = jnp.zeros_like(dk_acc)
        dv_acc[...] = jnp.zeros_like(dv_acc)

        def back_block(j, carry):
            sides = []
            for h in range(2):
                head = 2 * pair + h
                probs = jnp.exp(nt(ka[pair], qa[head, j]))
                grad_probs = nt(va[pair], dom[head, j])
                delta = jnp.sum(probs * grad_probs, axis=0, keepdims=True)
                grad_scores = (probs * (grad_probs - delta)).astype(BF16)
                dv_acc[...] += nn(probs.astype(BF16), dom[head, j])
                dk_acc[...] += nn(grad_scores, qa[head, j, :, :LANES])
                sides.append(nn(kt[pair], grad_scores))
            half_lane = LANES // 2
            turned = jnp.concatenate([sides[0][:half_lane], sides[1][half_lane:]], axis=0)
            dqkv[0, j, :, pair * LANES : (pair + 1) * LANES] = (jnp.transpose(turned) * 0.125).astype(BF16)
            return carry

        lax.fori_loop(0, 4, back_block, 0)
        for j in range(4):
            at = slice(j * rows, (j + 1) * rows)
            dqkv[1, j, :, pair * LANES : (pair + 1) * LANES] = dk_acc[at, :].astype(BF16)
            dqkv[2, j, :, pair * LANES : (pair + 1) * LANES] = dv_acc[at, :].astype(BF16)

    back_pair(0)
    back_pair(1)

    sum_a = Scatter(cp, part2, in_x, in_y, via_x, via_y, 54, place)

    def grad_in(r):
        blk = peer(r)
        left = jnp.concatenate([dqkv[c, blk] for c in range(3)], axis=1)
        for k in range(per_a):
            at = slice(k * slab_a, (k + 1) * slab_a)
            right = jnp.concatenate([w_attn[c * per_a + k] for c in range(3)], axis=0)
            value = nn(left, right)
            if r == 0:
                own[:, at] = value
            else:
                part2[r - 1, :, at] = value.astype(BF16)

    for r in (3, 1, 2):
        grad_in(r)
        sum_a.start(r)
    grad_in(0)

    my_cols = pl.ds(pl.multiple_of(s * local, local), local)
    for j in range(4):
        vec_grad[2:3, my_cols] += col_sum(dqkv[0, j].astype(F32))
        vec_grad[3:4, my_cols] += col_sum(dqkv[2, j].astype(F32))

    def attn_grads(c):
        turned = jnp.transpose(jnp.concatenate([dqkv[c, p] for p in range(4)], axis=0))
        for k in range(per_a):
            cols = jnp.concatenate([a_g[p, :, k * slab_a : (k + 1) * slab_a] for p in range(4)], axis=0)
            g_attn[c * per_a + k] = nn(turned, cols).astype(BF16)

    attn_grads(0)
    attn_grads(1)
    sum_a.relay_y()
    sum_a.relay_x()
    attn_grads(2)
    ga_in.wait_x()
    ga_in.wait_y()
    ga_in.wait_d()
    turned = jnp.transpose(jnp.concatenate([att[s, p] for p in range(4)], axis=0))
    for k in range(per_a):
        cols = jnp.concatenate([ga_g[p, :, k * slab_a : (k + 1) * slab_a] for p in range(4)], axis=0)
        g_attn[3 * per_a + k] = nn(turned, cols).astype(BF16)

    sum_o.wait()
    for k in range(per_f):
        at = slice(k * slab_f, (k + 1) * slab_f)
        total = out_part(s, k) + resid[:, at] + in_x2[:, at].astype(F32) + in_y2[:, at].astype(F32) + vec[7:8, at]
        out[:, at] = total.astype(BF16)

    sum_a.wait()

    def back_one(i, carry):
        at = pl.ds(pl.multiple_of(i * chunk, chunk), chunk)
        at_all = pl.ds(pl.multiple_of(s * rows + i * chunk, chunk), chunk)
        grad_a = own[at, :] + in_x[at, :].astype(F32) + in_y[at, :].astype(F32)
        masked = mask_col[at_all, :] > 0.0
        normed, inv_std = normalise(jnp.where(masked, vec[8:9, :], frames[at, :].astype(F32)))
        grad_x = gres[at, :] + norm_back(grad_a, normed, inv_std, vec[0:1, :])
        frames_grad[at, :] = jnp.where(masked, 0.0, grad_x)
        vec_grad[0:1, :] += col_sum(grad_a * normed)
        vec_grad[1:2, :] += col_sum(grad_a)
        vec_grad[8:9, :] += col_sum(jnp.where(masked, grad_x, 0.0))
        return carry

    lax.fori_loop(0, rows // chunk, back_one, 0)

    frames_in.sent()
    wp_in.sent()
    for copy in wp_cross:
        copy.wait_send()
    cot_in.sent()

    def att_sent(j, carry):
        att_x(j, s).wait_send()
        att_y(j, s).wait_send()
        att_relay(j, False)
        return carry

    lax.fori_loop(0, 4, att_sent, 0)
    for i, r in enumerate((3, 1, 2)):
        cp(gsend.at[r], gm.at[s], 39 + i, peer(r)).wait_send()
    ga_in.sent()
    sum_o.sent()
    sum_a.sent()


def run_layer(frames, mask_col, cot, seg_q, seg_k, vec, w_attn, w_ffn):
    rows, width = frames.shape
    group = 4 * rows
    hidden = w_ffn.shape[1]
    local = width // 4
    vmem = pl.BlockSpec(memory_space=pltpu.VMEM)
    block = (4, rows, width)
    scratch = [
        pltpu.VMEM(block, BF16),
        pltpu.VMEM(block, BF16),
        pltpu.VMEM(block, BF16),
        pltpu.VMEM((4, local, width), BF16),
        pltpu.VMEM((4, 4, rows, 2 * LANES), BF16),
        pltpu.VMEM((2, group, 2 * LANES), BF16),
        pltpu.VMEM((2, group, LANES), BF16),
        pltpu.VMEM((2, LANES, group), BF16),
        pltpu.VMEM((4, 4, rows, local), BF16),
        pltpu.VMEM(block, BF16),
        pltpu.VMEM((4, rows, hidden), BF16),
        pltpu.VMEM((4, rows, hidden), BF16),
        pltpu.VMEM((rows, width), F32),
        pltpu.VMEM((rows, width), F32),
        pltpu.VMEM((3, rows, width), BF16),
        pltpu.VMEM((3, rows, width), BF16),
        pltpu.VMEM((rows, width), BF16),
        pltpu.VMEM((rows, width), BF16),
        pltpu.VMEM((rows // 2, width), BF16),
        pltpu.VMEM((rows // 2, width), BF16),
        pltpu.VMEM((rows, width), BF16),
        pltpu.VMEM((rows, width), BF16),
        pltpu.VMEM((rows // 2, width), BF16),
        pltpu.VMEM((rows // 2, width), BF16),
        pltpu.VMEM((4, rows, local), BF16),
        pltpu.VMEM((4, rows, local), BF16),
        pltpu.VMEM((4, 4, rows, LANES), BF16),
        pltpu.VMEM(block, BF16),
        pltpu.VMEM((rows, width), F32),
        pltpu.VMEM((3, 4, rows, local), BF16),
        pltpu.VMEM((group, LANES), F32),
        pltpu.VMEM((group, LANES), F32),
        pltpu.SemaphoreType.DMA((60,)),
        pltpu.SemaphoreType.DMA((60,)),
    ]
    return pl.pallas_call(
        layer_kernel,
        out_shape=(
            jax.ShapeDtypeStruct((rows, width), BF16),
            jax.ShapeDtypeStruct((rows, width), F32),
            jax.ShapeDtypeStruct(vec.shape, F32),
            jax.ShapeDtypeStruct(w_attn.shape, BF16),
            jax.ShapeDtypeStruct(w_ffn.shape, BF16),
        ),
        in_specs=[vmem] * 8,
        out_specs=(vmem,) * 5,
        scratch_shapes=scratch,
        compiler_params=pltpu.CompilerParams(
            collective_id=0, has_side_effects=True, vmem_limit_bytes=60 * 1024 * 1024
        ),
    )(frames, mask_col, cot, seg_q, seg_k, vec, w_attn, w_ffn)


def per_device(
    frames,
    segment_ids,
    span_starts,
    cotangent,
    attn_master,
    attn_first,
    attn_second,
    ffn_master,
    ffn_first,
    ffn_second,
    vec_master,
    vec_first,
    vec_second,
):
    dp_count = lax.axis_size("dp")
    group = segment_ids.shape[1]

    def gather_slabs(master):
        shard = master.astype(BF16)
        if dp_count == SLABS:
            return lax.all_gather(shard, "dp", axis=0)
        whole = lax.all_gather(shard, "dp", axis=1, tiled=True)
        return whole.reshape(shard.shape[0], SLABS, -1).transpose(1, 0, 2)

    w_attn = gather_slabs(attn_master)
    w_ffn = gather_slabs(ffn_master)

    positions = lax.iota(jnp.int32, group)
    starts = span_starts[0]
    inside = (positions[:, None] >= starts[None, :]) & (positions[:, None] < starts[None, :] + SPAN)
    mask_col = jnp.any(inside, axis=1).astype(F32)[:, None]
    seg = segment_ids[0][:, None]
    lane = lax.broadcasted_iota(jnp.int32, (group, LANES), 1)
    first, second = seg == 0, seg == 1
    zero = jnp.zeros((), F32)
    seg_q = jnp.where(lane == 0, jnp.where(second, NEG_FILL, zero), jnp.where(lane == 1, jnp.where(first, NEG_FILL, zero), zero))
    seg_k = jnp.where(
        lane == 0,
        first.astype(F32),
        jnp.where(lane == 1, second.astype(F32), ((lane >= 2) & (lane <= 4)).astype(F32)),
    )
    output, frames_grad, vec_local, g_attn, g_ffn = run_layer(
        frames[0], mask_col, cotangent[0], seg_q.astype(BF16), seg_k.astype(BF16), vec_master, w_attn, w_ffn
    )

    def scatter_slabs(slabs):
        slabs = slabs.astype(F32)
        if dp_count == SLABS:
            return lax.psum_scatter(slabs, "dp", scatter_dimension=0, tiled=False)
        whole = slabs.transpose(1, 0, 2).reshape(slabs.shape[1], -1)
        return lax.psum_scatter(whole, "dp", scatter_dimension=1, tiled=True)

    attn_owned = scatter_slabs(g_attn)
    ffn_owned = scatter_slabs(g_ffn)
    owned_squares = jnp.sum(attn_owned * attn_owned) + jnp.sum(ffn_owned * ffn_owned)
    vec_grad, total_squares = lax.psum((vec_local, owned_squares), ("seq", "dp"))
    grad_norm = jnp.sqrt(total_squares + jnp.sum(vec_grad * vec_grad))
    clip = jnp.minimum(1.0, MAX_NORM / (grad_norm + 1e-06))
    attn_new, attn_first_new, attn_second_new = adam_step(
        attn_master, attn_first, attn_second, attn_owned * clip, RATE_ATTN, DECAY_RATE
    )
    ffn_new, ffn_first_new, ffn_second_new = adam_step(
        ffn_master, ffn_first, ffn_second, ffn_owned * clip, RATE_FFN, DECAY_RATE
    )
    vec_new, vec_first_new, vec_second_new = adam_step(
        vec_master, vec_first, vec_second, vec_grad * clip, RATE_VEC, 0.0
    )
    return (
        output[None],
        frames_grad[None],
        grad_norm,
        attn_new,
        attn_first_new,
        attn_second_new,
        attn_new.astype(BF16),
        ffn_new,
        ffn_first_new,
        ffn_second_new,
        ffn_new.astype(BF16),
        vec_new,
        vec_first_new,
        vec_second_new,
    )


def solution(mesh):
    return jax.shard_map(
        per_device,
        mesh=mesh,
        in_specs=(
            P("dp", "seq", None),
            P("dp", None),
            P("dp", None),
            P("dp", "seq", None),
            P("seq", "dp"),
            P("seq", "dp"),
            P("seq", "dp"),
            P("seq", "dp"),
            P("seq", "dp"),
            P("seq", "dp"),
            P(),
            P(),
            P(),
        ),
        out_specs=(
            P("dp", "seq", None),
            P("dp", "seq", None),
            P(),
            P("seq", "dp"),
            P("seq", "dp"),
            P("seq", "dp"),
            P("seq", "dp"),
            P("seq", "dp"),
            P("seq", "dp"),
            P("seq", "dp"),
            P("seq", "dp"),
            P(),
            P(),
            P(),
        ),
        check_vma=False,
    )
```

time: 744 us -> 457 us (0.61); the launches traced: 733 us -> 456 us
  Pallas kernels: 0 us -> 164 us
  waiting for transfers between devices: 353 us -> 204 us
  local copies, waits for them, and re-layouts: 117 us -> 2.85 us
  matrix products: 109 us -> 0 us
  blocking collectives: 63.9 us -> 38.7 us
  other arithmetic: 49.7 us -> 28.7 us
  starting transfers between devices: 20 us -> 0.16 us
    pallas_call x0 -> x1, Pallas kernels: none -> 164 us  [run_layer(): pl.pallas_call(layer_kernel, out_shape=(jax.ShapeDtypeStruct((rows, width...]
    dot_general x26 -> x0, matrix products: 109 us -> none  [the longest x3 14.1 us: cross_rows(): jnp.einsum('ti,tj->ij', left, right, preferred_element_type=jnp.float32)]
    all_to_all x5 -> x0, waiting for transfers between devices: 89.9 us -> none  [the longest x1 43.1 us: per_device(): lax.all_to_all(qkv_low, 'seq', split_axis=2, concat_axis=0, tiled=True)]
    all_gather x6 -> x2, waiting for transfers between devices: 145 us -> 74.4 us  [gather_slabs(): return lax.all_gather(shard, 'dp', axis=0)]
    unnamed x109 -> x26, local copies, waits for them, and re-layouts: 33.5 us -> 1.82 us
    reshape x5 -> x0, local copies, waits for them, and re-layouts: 31.3 us -> none  [the longest x2 27 us: lay_out(): whole.reshape(seq_count, dp_count, rows, cols).transpose(0, 2, 1, 3)]
    all_to_all x1 -> x0, blocking collectives: 25.2 us -> none  [per_device(): lax.all_to_all(grad_heads_qkv, 'seq', split_axis=0, concat_axis=2, tiled=...]
    all_to_all x5 -> x0, starting transfers between devices: 19.2 us -> none  [the longest x1 4.63 us: per_device(): lax.all_to_all(act_low, 'seq', split_axis=1, concat_axis=0, tiled=True)]
  transfers between devices with their start and end apart: 13 -> 4, of which waited for: 9 -> 4; matrix products, arithmetic and copies ran while one was open for 26% -> 3% of each run, Pallas kernels for 0% -> 0%
where the time goes in v1:
time: 457 us; the launch traced here: 456 us
  waiting for transfers between devices  204 us (45%)
  Pallas kernels  164 us (36%)
  blocking collectives  38.7 us (8%)
  other arithmetic  28.7 us (6%)
  between operations  17.7 us (4%)
    pallas_call x1, Pallas kernels, run_layer(): pl.pallas_call(layer_kernel, out_shape=(jax.ShapeDtypeStruct((rows, width...  164 us
    reduce_scatter x2, waiting for transfers between devices, scatter_slabs(): return lax.psum_scatter(slabs, 'dp', scatter_dimension=0, tiled=False)  130 us
    all_gather x2, waiting for transfers between devices, gather_slabs(): return lax.all_gather(shard, 'dp', axis=0)  74.4 us
    psum x1, blocking collectives, per_device(): lax.psum((vec_local, owned_squares), ('seq', 'dp'))  38.7 us
    convert_element_type x2, other arithmetic, scatter_slabs(): slabs = slabs.astype(F32)  10.2 us
  transfers between devices with their start and end apart: 4, of which 4 were waited for; matrix products, arithmetic and copies ran while one was open for 3% of the time, Pallas kernels for 0%

profile of v1, /device:TPU:0, one launch (start us, length us, event | category | flops | bytes accessed | tf_op | source)
XLA Modules:
  0.0 456.3 jit_solution(6966165667358115558)
XLA Ops:
  7.2 1.8 convert_element_type.72
  9.1 2.1 convert_element_type.73
  11.2 0.7 add_bitcast_fusion
  11.9 0.8 fusion.5
  12.7 1.0 copy.28.mask_col
  13.7 0.7 compare_convert_fusion
  14.4 0.7 compare_select_fusion.1
  15.1 1.4 select_convert_fusion
  16.5 25.5 %all-gather.5.cloned.1.call-done = bf16[2048,512]{1,0:T(8,128)(2,1)} async-done(((bf16[256,512]{1,0:T(8,128)(2,1)}), bf16[2048,512]{1,0:T(8,128)(2,1)}) %all-gather.5.cloned.1.call-update) | async-done | bytes 2097168 | tf_op jit(solution)/shard_map/all_gather | solution.py:731
  42.0 48.8 %all-gather.7.cloned.1.call-done = bf16[8192,256]{1,0:T(8,128)(2,1)} async-done(((bf16[1024,256]{1,0:T(8,128)(2,1)}), bf16[8192,256]{1,0:T(8,128)(2,1)}) %all-gather.7.cloned.1.call-update) | async-done | bytes 4194320 | tf_op jit(solution)/shard_map/all_gather | solution.py:731
  90.9 163.8 %shard_map.236 = (bf16[256,1024]{1,0:T(8,128)(2,1)}, f32[256,1024]{1,0:T(8,128)}, f32[13,1024]{1,0:T(8,128)}, bf16[8,256,512]{2,1,0:T(8,128)(2,1)}, bf16[8,1024,256]{2,1,0:T(8,128)(2,1)}) custom-call(bf16[256,1024]{1,0:T(8,128)(2,1)} %bitcast.31, f32[1024,1]{1,0:T(8,128)} %copy.28.mask_col, bf16[256,1024]{1,0:T(8,128)(2,1)} %bitcast.32, ...), custom_call_target="tpu_custom_call" | custom-call | tf_op jit(solution)/shard_map/pallas_call | solution.py:692
  254.7 4.1 convert_element_type.74
  258.9 6.2 %convert_element_type.75 = f32[8,1024,256]{2,1,0:T(8,128)} convert(bf16[8,1024,256]{2,1,0:T(8,128)(2,1)} %get-tuple-element.22) | non-fusion elementwise | flops 2097152 | bytes 12582912 | tf_op jit(solution)/shard_map/convert_element_type | solution.py:757
  265.1 41.7 %reduce-scatter.3.cloned.1.call-done = f32[1,256,512]{2,1,0:T(8,128)} async-done(((f32[8,256,512]{2,1,0:T(8,128)}), f32[1,256,512]{2,1,0:T(8,128)}) %reduce-scatter.3.cloned.1.call-update) | async-done | bytes 524304 | tf_op jit(solution)/shard_map/reduce_scatter | solution.py:759
  306.8 1.8 multiply_reduce_fusion.1
  308.6 88.2 %reduce-scatter.5.cloned.1.call-done = f32[1,1024,256]{2,1,0:T(8,128)} async-done(((f32[8,1024,256]{2,1,0:T(8,128)}), f32[1,1024,256]{2,1,0:T(8,128)}) %reduce-scatter.5.cloned.1.call-update) | async-done | bytes 1048592 | tf_op jit(solution)/shard_map/reduce_scatter | solution.py:759
  396.7 2.2 multiply_reduce_fusion
  400.2 38.7 %all-reduce = (f32[]{:T(128)}, f32[13,1024]{1,0:T(8,128)S(1)}) all-reduce(f32[]{:T(128)S(6)} %add.70, f32[13,1024]{1,0:T(8,128)S(1)} %copy-done.9), channel_id=1, replica_groups=mesh['seq'=4,'dp'=8] {'seq','dp'}, use_global_device_ids=true, to_apply=%region_5.6 | all-reduce | flops 13313 | bytes 106504 | tf_op jit(solution)/shard_map/psum | solution.py:766
  438.9 0.6 multiply_reduce_fusion.2
  441.0 0.7 multiply_subtract_fusion.2
  441.7 2.7 fusion.11
  444.5 2.4 fusion.8
  446.8 0.8 copy.31
  447.6 1.0 copy.32
  (35 shorter events, 0.3 us)
Async XLA Ops:
  7.2 34.8 %all-gather.5.cloned.1.call-start = ((), (), s32[]{:S(2)}) async-start(), calls=%async_computation.4 | async-start | bytes 2359296 | tf_op jit(solution)/shard_map/all_gather | solution.py:731
  9.0 81.8 %all-gather.7.cloned.1.call-start = ((), (), s32[]{:S(2)}) async-start(), calls=%async_computation.5 | async-start | bytes 4718592 | tf_op jit(solution)/shard_map/all_gather | solution.py:731
  11.2 295.6 %reduce-scatter.3.cloned.1.call-start = ((), (), s32[]{:S(2)}) async-start(), calls=%async_computation.2 | async-start | bytes 4718592 | tf_op jit(solution)/shard_map/reduce_scatter | solution.py:759
  258.8 137.9 %reduce-scatter.5.cloned.1.call-start = ((), (), s32[]{:S(2)}) async-start(), calls=%async_computation.3 | async-start | bytes 9437184 | tf_op jit(solution)/shard_map/reduce_scatter | solution.py:759
  265.0 135.2 %copy-start.9 = (f32[13,1024]{1,0:T(8,128)S(1)}, f32[13,1024]{1,0:T(8,128)}, u32[]{:S(2)}) copy-start(f32[13,1024]{1,0:T(8,128)} %get-tuple-element.23) | copy-start | bytes 159748
  265.0 175.9 %copy-start.8 = (f32[13,1024]{1,0:T(8,128)S(1)}, f32[13,1024]{1,0:T(8,128)}, u32[]{:S(2)}) copy-start(f32[13,1024]{1,0:T(8,128)} %vec.1) | copy-start | bytes 159748
  265.0 175.9 %copy-start.10 = (f32[13,1024]{1,0:T(8,128)S(1)}, f32[13,1024]{1,0:T(8,128)}, u32[]{:S(2)}) copy-start(f32[13,1024]{1,0:T(8,128)} %param.24) | copy-start | bytes 159748
  265.0 175.9 %copy-start.11 = (f32[13,1024]{1,0:T(8,128)S(1)}, f32[13,1024]{1,0:T(8,128)}, u32[]{:S(2)}) copy-start(f32[13,1024]{1,0:T(8,128)} %param.25) | copy-start | bytes 159748
  265.0 176.7 %copy-start.2 = (f32[256,512]{1,0:T(8,128)S(1)}, f32[256,512]{1,0:T(8,128)}, u32[]{:S(2)}) copy-start(f32[256,512]{1,0:T(8,128)} %param.17) | copy-start | bytes 1572868
  265.0 176.6 %copy-start.6 = (f32[256,512]{1,0:T(8,128)S(1)}, f32[256,512]{1,0:T(8,128)}, u32[]{:S(2)}) copy-start(f32[256,512]{1,0:T(8,128)} %param.18) | copy-start | bytes 1572868
  265.1 179.3 %copy-start = (f32[1024,256]{1,0:T(8,128)S(1)}, f32[1024,256]{1,0:T(8,128)}, u32[]{:S(2)}) copy-start(f32[1024,256]{1,0:T(8,128)} %param.20) | copy-start | bytes 3145732
  396.7 47.7 %copy-start.1 = (f32[1,1024,256]{2,1,0:T(8,128)S(1)}, f32[1,1024,256]{2,1,0:T(8,128)}, u32[]{:S(2)}) copy-start(f32[1,1024,256]{2,1,0:T(8,128)} %reduce-scatter.5.cloned.1.call-done) | copy-start | bytes 3145732
  441.0 3.4 copy-start.3
  441.0 3.4 copy-start.4
  444.4 2.4 copy-start.7
  444.4 3.2 copy-start.5
Sparse Core Ops, SparseCore 0:
  10.2 31.7 all-gather.4
  44.2 46.6 all-gather.6
  258.9 47.7 reduce-scatter.2
  308.9 87.7 reduce-scatter.4

commit v2 on v1

--- a/solution.py
+++ b/solution.py
@@ -24,6 +24,7 @@
 
 SLABS = 8
 LANES = 128
+VMEM_LIMIT = 62 * 1024 * 1024
 F32 = jnp.float32
 BF16 = jnp.bfloat16
 MESH = pl.DeviceIdType.MESH
@@ -159,55 +160,247 @@
             copy.wait_send()
 
 
-def layer_kernel(
-    frames,
-    mask_col,
-    cot,
-    seg_q,
-    seg_k,
-    vec,
-    w_attn,
-    w_ffn,
-    out,
-    frames_grad,
-    vec_grad,
-    g_attn,
-    g_ffn,
-    fr_g,
-    cot_g,
-    a_g,
-    wp,
-    qa,
-    ka,
-    va,
-    kt,
-    att,
-    b_g,
-    act_g,
-    gp_g,
-    resid,
-    own,
-    part,
-    part2,
-    in_x,
-    in_y,
-    via_x,
-    via_y,
-    in_x2,
-    in_y2,
-    via_x2,
-    via_y2,
-    gsend,
-    gm,
-    dom,
-    ga_g,
-    gres,
-    dqkv,
-    dk_acc,
-    dv_acc,
-    send_sem,
-    recv_sem,
-):
+class Line:
+    def __init__(self, cp_dp, buf, base, chip, core, chips):
+        self.cp, self.buf, self.b = cp_dp, buf, base
+        self.z, self.core, self.n = chip, core, chips
+
+    def c(self, shard, kind, to):
+        at = 2 * shard + self.core
+        return self.cp(self.buf.at[at], self.buf.at[at], self.b + kind * self.n + shard, to)
+
+    def up(self, shard):
+        return self.c(shard, 0, 2 * (self.z + 1) + self.core)
+
+    def down(self, shard):
+        return self.c(shard, 1, 2 * (self.z - 1) + self.core)
+
+    def across(self, shard):
+        return self.c(shard, 2, 2 * self.z + 1 - self.core)
+
+    def start_up(self):
+        @pl.when(self.z < self.n - 1)
+        def _():
+            self.up(self.z).start()
+
+    def start_down(self):
+        @pl.when(self.z > 0)
+        def _():
+            self.down(self.z).start()
+
+    def start(self):
+        self.start_up()
+        self.start_down()
+        self.across(self.z).start()
+
+    def step(self, k):
+        low, high = self.z - k, self.z + k
+
+        @pl.when(low >= 0)
+        def _():
+            self.c(low, 0, 2 * self.z + 1 - self.core).wait_recv()
+
+            @pl.when(self.z < self.n - 1)
+            def _():
+                self.up(low).start()
+
+            self.across(low).start()
+
+        @pl.when(high < self.n)
+        def _():
+            self.c(high, 1, 2 * self.z + 1 - self.core).wait_recv()
+
+            @pl.when(self.z > 0)
+            def _():
+                self.down(high).start()
+
+            self.across(high).start()
+
+    def crossed(self, shard):
+        other = 1 - self.core
+        ref = self.buf.at[2 * shard + other]
+        self.cp(ref, ref, self.b + 2 * self.n + shard, 2 * self.z + other).wait_recv()
+
+    def sent(self):
+        for shard in range(self.n):
+            self.across(shard).wait_send()
+
+            @pl.when(jnp.logical_and(shard <= self.z, self.z < self.n - 1))
+            def _(shard=shard):
+                self.up(shard).wait_send()
+
+            @pl.when(jnp.logical_and(shard >= self.z, self.z > 0))
+            def _(shard=shard):
+                self.down(shard).wait_send()
+
+
+class LineSum:
+    def __init__(self, cp_dp, part, cross, landed, base, chip, core, chips):
+        self.cp, self.part, self.cross, self.landed, self.b = cp_dp, part, cross, landed, base
+        self.z, self.core, self.n = chip, core, chips
+
+    def mine(self, shard):
+        return 2 * shard + self.core
+
+    def across(self, shard):
+        src = self.part.at[2 * shard + 1 - self.core]
+        return self.cp(src, self.cross.at[shard], self.b + shard, 2 * self.z + 1 - self.core)
+
+    def up(self, shard):
+        src = self.part.at[self.mine(shard)]
+        return self.cp(src, self.landed.at[shard + 1], self.b + self.n + shard, 2 * (self.z + 1) + self.core)
+
+    def down(self, shard):
+        src = self.part.at[self.mine(shard)]
+        return self.cp(src, self.landed.at[shard], self.b + 2 * self.n + shard, 2 * (self.z - 1) + self.core)
+
+    def start(self, shard):
+        self.across(shard).start()
+
+    def add(self, shard, ref):
+        size = min(256, ref.shape[0])
+
+        def one(i, carry):
+            at = pl.ds(pl.multiple_of(i * size, size), size)
+            total = self.part[self.mine(shard), at, :].astype(F32) + ref[at, :].astype(F32)
+            self.part[self.mine(shard), at, :] = total.astype(BF16)
+            return carry
+
+        lax.fori_loop(0, ref.shape[0] // size, one, 0)
+
+    def fold(self, shard):
+        self.across(shard).wait_recv()
+        self.add(shard, self.cross.at[shard])
+
+    def step(self, k):
+        if k > self.n - 2:
+            return
+        up, down = self.n - 1 - k + self.z, k - (self.n - 1 - self.z)
+
+        @pl.when(k >= self.z)
+        def _():
+            @pl.when(k > self.z)
+            def _():
+                self.up(up + 1).wait_send()
+
+            @pl.when(self.z > 0)
+            def _():
+                self.up(up).wait_recv()
+                self.add(up, self.landed.at[up + 1])
+
+            self.up(up).start()
+
+        @pl.when(k >= self.n - 1 - self.z)
+        def _():
+            @pl.when(k > self.n - 1 - self.z)
+            def _():
+                self.down(down - 1).wait_send()
+
+            @pl.when(self.z < self.n - 1)
+            def _():
+                self.down(down).wait_recv()
+                self.add(down, self.landed.at[down])
+
+            self.down(down).start()
+
+    def finish(self, owned):
+        owned[...] = self.part[self.mine(self.z)].astype(F32)
+
+        @pl.when(self.z > 0)
+        def _():
+            self.up(self.z).wait_recv()
+            owned[...] += self.landed[self.z + 1].astype(F32)
+
+        @pl.when(self.z < self.n - 1)
+        def _():
+            self.down(self.z).wait_recv()
+            owned[...] += self.landed[self.z].astype(F32)
+
+    def sent(self):
+        for shard in range(self.n):
+            self.across(shard).wait_send()
+
+        @pl.when(self.z < self.n - 1)
+        def _():
+            self.up(self.z + 1).wait_send()
+
+        @pl.when(self.z > 0)
+        def _():
+            self.down(self.z - 1).wait_send()
+
+
+class Everyone:
+    def __init__(self, cp_any, plane, line, base, s, chip, core, chips):
+        self.cp, self.plane, self.line, self.b = cp_any, plane, line, base
+        self.s, self.z, self.core, self.n = s, chip, core, chips
+        self.me = 2 * s + core
+
+    def to_plane(self, o):
+        p = lax.rem(self.me + o, 8)
+        return self.cp(self.plane.at[self.me], self.plane.at[self.me], self.b + o, p // 2, 2 * self.z + lax.rem(p, 2))
+
+    def from_plane(self, o):
+        p = lax.rem(self.me - o + 8, 8)
+        return self.cp(self.plane.at[p], self.plane.at[p], self.b + o, p // 2, 2 * self.z + lax.rem(p, 2))
+
+    def to_line(self, o):
+        p = lax.rem(self.z + o, self.n)
+        return self.cp(self.line.at[self.z], self.line.at[self.z], self.b + 7 + o, self.s, 2 * p + self.core)
+
+    def from_line(self, o):
+        p = lax.rem(self.z - o + self.n, self.n)
+        return self.cp(self.line.at[p], self.line.at[p], self.b + 7 + o, self.s, 2 * p + self.core)
+
+    def start(self, value):
+        self.plane[self.me] = value
+        for o in range(1, 8):
+            self.to_plane(o).start()
+
+    def middle(self):
+        for o in range(1, 8):
+            self.from_plane(o).wait_recv()
+        total = self.plane[0]
+        for p in range(1, 8):
+            total = total + self.plane[p]
+        self.line[self.z] = total
+        for o in range(1, self.n):
+            self.to_line(o).start()
+
+    def end(self):
+        for o in range(1, self.n):
+            self.from_line(o).wait_recv()
+        total = self.line[0]
+        for p in range(1, self.n):
+            total = total + self.line[p]
+        return total
+
+    def sent(self):
+        for o in range(1, 8):
+            self.to_plane(o).wait_send()
+        for o in range(1, self.n):
+            self.to_line(o).wait_send()
+
+
+def layer_kernel(inside, chips, *refs):
+    refs = list(refs)
+
+    def take(count):
+        head = refs[:count]
+        del refs[:count]
+        return head
+
+    frames, mask_col, cot, seg_q, seg_k, vec, attn_src, ffn_src = take(8)
+    if inside:
+        out, frames_grad, vec_out, norm_out, attn_owned, ffn_owned = take(6)
+    else:
+        out, frames_grad, early, late, g_attn, g_ffn = take(6)
+        w_attn, w_ffn = attn_src, ffn_src
+    fr_g, cot_g, a_g, wp, qa, ka, va, kt, att, b_g, gp_g = take(11)
+    act_g = fr_g
+    resid, own, part, in_x, in_y, via_x, via_y, in_x2, in_y2, via_x2, via_y2 = take(11)
+    gsend, gm, dom, ga_g, gres, dqkv, dk_acc, dv_acc, send_sem, recv_sem, local_sem = take(11)
+    if inside:
+        w_attn, w_ffn, g_attn, g_ffn, cross_a, cross_f, landed_a, landed_f, early, late, planes, lines = take(12)
     s = lax.axis_index("seq")
     d = lax.axis_index("dp")
     core = lax.rem(d, 2)
@@ -231,15 +424,24 @@
             device_id_type=MESH,
         )
 
-    def cp_sib(src, dst, i):
+    def cp_any(src, dst, i, to_seq, to_dp):
         return pltpu.make_async_remote_copy(
             src_ref=src,
             dst_ref=dst,
             send_sem=send_sem.at[i],
             recv_sem=recv_sem.at[i],
-            device_id=(s, sib),
+            device_id=(to_seq, to_dp),
             device_id_type=MESH,
         )
+
+    def cp_dp(src, dst, i, to):
+        return cp_any(src, dst, i, s, to)
+
+    def cp_sib(src, dst, i):
+        return cp_any(src, dst, i, s, sib)
+
+    def no_step(k):
+        return None
 
     rows = frames.shape[0]
     width = frames.shape[1]
@@ -251,27 +453,55 @@
     tile = 256
     chunk = 32
 
+    cot_load = pltpu.make_async_copy(cot, cot_g.at[s], local_sem.at[0])
+    cot_load.start()
+    chip = d // 2
+    loads = []
+    if inside:
+        loads = [pltpu.make_async_copy(attn_src, own.at[:, :slab_a], local_sem.at[1])]
+        for i, spot in enumerate((dk_acc, dv_acc)):
+            at = slice(i * LANES, (i + 1) * LANES)
+            loads.append(pltpu.make_async_copy(ffn_src.at[:, at], spot, local_sem.at[2 + i]))
+        for load in loads:
+            load.start()
+
     barrier = pltpu.get_barrier_semaphore()
-    for to in (px, py, pd):
-        pl.semaphore_signal(barrier, inc=1, device_id=(to, d), device_id_type=MESH)
-    pl.semaphore_signal(barrier, inc=1, device_id=(s, sib), device_id_type=MESH)
-    pl.semaphore_wait(barrier, 4)
+    if inside:
+        for o in range(1, 8):
+            p = lax.rem(2 * s + core + o, 8)
+            to = (p // 2, 2 * chip + lax.rem(p, 2))
+            pl.semaphore_signal(barrier, inc=1, device_id=to, device_id_type=MESH)
+        for o in range(1, chips):
+            to = (s, 2 * lax.rem(chip + o, chips) + core)
+            pl.semaphore_signal(barrier, inc=1, device_id=to, device_id_type=MESH)
+        pl.semaphore_wait(barrier, 6 + chips)
+    else:
+        for to in (px, py, pd):
+            pl.semaphore_signal(barrier, inc=1, device_id=(to, d), device_id_type=MESH)
+        pl.semaphore_signal(barrier, inc=1, device_id=(s, sib), device_id_type=MESH)
+        pl.semaphore_wait(barrier, 4)
 
     fr_g[s] = frames[...]
     frames_in = Gather(cp, fr_g, 0, place, 0, rows)
     frames_in.start()
-
-    cot_g[s] = cot[...]
     cot_in = Gather(cp, cot_g, 15, place, 0, rows)
-    for i in range(per_a):
-        wp[s, :, i * slab_a : (i + 1) * slab_a] = w_attn[3 * per_a + i]
+    attn_step = ffn_step = no_step
+    if inside:
+        line_a = Line(cp_dp, w_attn, 60, chip, core, chips)
+        line_f = Line(cp_dp, w_ffn, 60 + 3 * chips, chip, core, chips)
+        loads[0].wait()
+        w_attn[d] = own[:, :slab_a].astype(BF16)
+        line_a.start()
+        attn_step, ffn_step = line_a.step, line_f.step
     half = rows // 2
     wp_off = pl.multiple_of(core * half, half)
     wp_in = Gather(cp, wp, 6, place, wp_off, half)
     wp_cross = [
         cp_sib(wp.at[p, pl.ds(wp_off, half)], wp.at[p, pl.ds(wp_off, half)], 12 + i) for i, p in enumerate((px, py, pd))
     ]
-    vec_grad[...] = jnp.zeros_like(vec_grad)
+    early[...] = jnp.zeros_like(early)
+    late[...] = jnp.zeros_like(late)
+    half = rows // 2
 
     lane = lax.broadcasted_iota(jnp.int32, (rows, LANES), 1)
     low_head = lane < LANES // 2
@@ -291,6 +521,8 @@
             return carry
 
         lax.fori_loop(0, rows // chunk, norm_rows, 0)
+
+    def project_in(blk):
         a = a_g[blk]
         at_all = pl.ds(pl.multiple_of(blk * rows, rows), rows)
         q = (nt(a, weight_rows(0, per_a, 0, local)) + q_bias).astype(BF16).astype(F32) * 0.125
@@ -311,15 +543,31 @@
             va[pair, at_all, :] = v[:, pair * LANES : (pair + 1) * LANES]
 
     enter(s)
+    if inside:
+        for i, spot in enumerate((dk_acc, dv_acc)):
+            loads[1 + i].wait()
+            w_ffn[d, :, i * LANES : (i + 1) * LANES] = spot[...].astype(BF16)
+    attn_step(1)
     frames_in.relay()
-    wp_in.start()
+    attn_step(2)
     frames_in.wait_x()
     enter(px)
     frames_in.wait_y()
     enter(py)
+    attn_step(3)
+    if inside:
+        line_f.start()
     frames_in.wait_d()
     enter(pd)
+    if inside:
+        for shard in range(chips):
+            line_a.crossed(shard)
+    for i in range(per_a):
+        wp[s, :, i * slab_a : (i + 1) * slab_a] = w_attn[3 * per_a + i]
+    wp_in.start()
+    lax.fori_loop(0, 4, lambda j, carry: (project_in(j), carry)[1], 0)
     wp_in.relay()
+    cot_load.wait()
     cot_in.start()
 
     def att_x(j, slot):
@@ -378,7 +626,9 @@
 
         return carry
 
-    lax.fori_loop(0, 4, attend, 0)
+    lax.fori_loop(0, 3, attend, 0)
+    ffn_step(1)
+    lax.fori_loop(3, 4, attend, 0)
     att_relay(3, True)
     wp_in.wait_x()
     wp_cross[0].start()
@@ -426,7 +676,13 @@
         lax.fori_loop(0, rows // chunk, norm_rows, 0)
         return carry
 
-    lax.fori_loop(0, 4, project, 0)
+    lax.fori_loop(0, 3, project, 0)
+    ffn_step(2)
+    lax.fori_loop(3, 4, project, 0)
+    ffn_step(3)
+    if inside:
+        for shard in range(chips):
+            line_f.crossed(shard)
 
     def feed(r):
         blk = peer(r)
@@ -442,7 +698,7 @@
             density = jnp.exp(-0.5 * pre * pre) * 0.3989422804014327
             grad_pre = ((cdf + pre * density) * grad_act).astype(BF16)
             gp_g[blk, :, at] = grad_pre
-            vec_grad[pl.ds(9 + s, 1), at] += col_sum(grad_pre.astype(F32))
+            early[pl.ds(4 + s, 1), at] += col_sum(grad_pre.astype(F32))
             return carry
 
         lax.fori_loop(0, w_ffn.shape[1] // tile, hidden_tile, 0)
@@ -459,6 +715,7 @@
     cot_in.wait_x()
     cot_in.wait_y()
     cot_in.wait_d()
+    frames_in.sent()
     feed(3)
     sum_b.start(3)
     feed(1)
@@ -474,15 +731,15 @@
         at = pl.ds(pl.multiple_of(i * chunk, chunk), chunk)
         grad_b = own[at, :] + in_x[at, :].astype(F32) + in_y[at, :].astype(F32)
         normed, inv_std = normalise(resid[at, :])
-        grad_y = cot[at, :].astype(F32)
+        grad_y = cot_g[s, at, :].astype(F32)
         grad_resid = grad_y + norm_back(grad_b, normed, inv_std, vec[5:6, :])
         gres[at, :] = grad_resid
         low = grad_resid.astype(BF16)
         ga_g[s, at, :] = low
-        vec_grad[4:5, :] += col_sum(low.astype(F32))
-        vec_grad[5:6, :] += col_sum(grad_b * normed)
-        vec_grad[6:7, :] += col_sum(grad_b)
-        vec_grad[7:8, :] += col_sum(grad_y)
+        early[0:1, :] += col_sum(low.astype(F32))
+        early[1:2, :] += col_sum(grad_b * normed)
+        early[2:3, :] += col_sum(grad_b)
+        early[3:4, :] += col_sum(grad_y)
         return carry
 
     lax.fori_loop(0, rows // chunk, back_two, 0)
@@ -515,6 +772,16 @@
         return carry
 
     lax.fori_loop(0, w_ffn.shape[1] // tile, ffn_grads, 0)
+    sum_step = no_step
+    if inside:
+        sum_f = LineSum(cp_dp, g_ffn, cross_f, landed_f, 60 + 6 * chips, chip, core, chips)
+        sum_g = LineSum(cp_dp, g_attn, cross_a, landed_a, 60 + 9 * chips, chip, core, chips)
+        all_early = Everyone(cp_any, planes.at[0], lines.at[0], 60 + 12 * chips, s, chip, core, chips)
+        all_late = Everyone(cp_any, planes.at[1], lines.at[1], 67 + 13 * chips, s, chip, core, chips)
+        sum_step = sum_f.step
+        for shard in range(chips):
+            sum_f.start(shard)
+        all_early.start(early[...])
 
     for i, r in enumerate((3, 1, 2)):
         cp(gsend.at[r], gm.at[peer(r)], 39 + i, peer(r)).wait_recv()
@@ -527,9 +794,15 @@
         return carry
 
     lax.fori_loop(0, 4, spread, 0)
+    if inside:
+        for shard in range(chips):
+            sum_f.fold(shard)
+    sum_step(0)
     ga_in.relay()
     sum_o.relay_y()
     sum_o.relay_x()
+    if inside:
+        all_early.middle()
 
     def back_pair(pair):
         dk_acc[...] = jnp.zeros_like(dk_acc)
@@ -558,9 +831,12 @@
             dqkv[2, j, :, pair * LANES : (pair + 1) * LANES] = dv_acc[at, :].astype(BF16)
 
     back_pair(0)
+    sum_step(1)
     back_pair(1)
-
-    sum_a = Scatter(cp, part2, in_x, in_y, via_x, via_y, 54, place)
+    sum_step(2)
+
+    sum_o.sent()
+    sum_a = Scatter(cp, part, in_x, in_y, via_x, via_y, 54, place)
 
     def grad_in(r):
         blk = peer(r)
@@ -572,7 +848,13 @@
             if r == 0:
                 own[:, at] = value
             else:
-                part2[r - 1, :, at] = value.astype(BF16)
+                part[r - 1, :, at] = value.astype(BF16)
+
+    sum_o.wait()
+    for k in range(per_f):
+        at = slice(k * slab_f, (k + 1) * slab_f)
+        total = out_part(s, k) + resid[:, at] + in_x2[:, at].astype(F32) + in_y2[:, at].astype(F32) + vec[7:8, at]
+        out[:, at] = total.astype(BF16)
 
     for r in (3, 1, 2):
         grad_in(r)
@@ -581,8 +863,8 @@
 
     my_cols = pl.ds(pl.multiple_of(s * local, local), local)
     for j in range(4):
-        vec_grad[2:3, my_cols] += col_sum(dqkv[0, j].astype(F32))
-        vec_grad[3:4, my_cols] += col_sum(dqkv[2, j].astype(F32))
+        late[2:3, my_cols] += col_sum(dqkv[0, j].astype(F32))
+        late[3:4, my_cols] += col_sum(dqkv[2, j].astype(F32))
 
     def attn_grads(c):
         turned = jnp.transpose(jnp.concatenate([dqkv[c, p] for p in range(4)], axis=0))
@@ -603,12 +885,13 @@
         cols = jnp.concatenate([ga_g[p, :, k * slab_a : (k + 1) * slab_a] for p in range(4)], axis=0)
         g_attn[3 * per_a + k] = nn(turned, cols).astype(BF16)
 
-    sum_o.wait()
-    for k in range(per_f):
-        at = slice(k * slab_f, (k + 1) * slab_f)
-        total = out_part(s, k) + resid[:, at] + in_x2[:, at].astype(F32) + in_y2[:, at].astype(F32) + vec[7:8, at]
-        out[:, at] = total.astype(BF16)
-
+    if inside:
+        for shard in range(chips):
+            sum_g.start(shard)
+        sum_f.finish(ffn_owned)
+        for shard in range(chips):
+            sum_g.fold(shard)
+        sum_g.step(0)
     sum_a.wait()
 
     def back_one(i, carry):
@@ -619,14 +902,36 @@
         normed, inv_std = normalise(jnp.where(masked, vec[8:9, :], frames[at, :].astype(F32)))
         grad_x = gres[at, :] + norm_back(grad_a, normed, inv_std, vec[0:1, :])
         frames_grad[at, :] = jnp.where(masked, 0.0, grad_x)
-        vec_grad[0:1, :] += col_sum(grad_a * normed)
-        vec_grad[1:2, :] += col_sum(grad_a)
-        vec_grad[8:9, :] += col_sum(jnp.where(masked, grad_x, 0.0))
+        late[0:1, :] += col_sum(grad_a * normed)
+        late[1:2, :] += col_sum(grad_a)
+        late[4:5, :] += col_sum(jnp.where(masked, grad_x, 0.0))
         return carry
 
     lax.fori_loop(0, rows // chunk, back_one, 0)
-
-    frames_in.sent()
+    if inside:
+        sum_g.step(1)
+        sum_g.step(2)
+        sum_g.finish(attn_owned)
+        late[5:6, :slab_a] = col_sum(attn_owned[...] * attn_owned[...])
+        late[5:6, slab_a : slab_a + slab_f] = col_sum(ffn_owned[...] * ffn_owned[...])
+        all_late.start(late[...])
+        whole_early = all_early.end()
+        all_late.middle()
+        whole_late = all_late.end()
+        vec_out[0:4, :] = whole_late[0:4]
+        vec_out[4:8, :] = whole_early[0:4]
+        vec_out[8:9, :] = whole_late[4:5]
+        vec_out[9:13, :] = whole_early[4:8]
+        vec_square = vec_out[...] * vec_out[...]
+        total = jnp.sum(col_sum(vec_square) + whole_late[5:6], axis=1, keepdims=True)
+        norm_out[...] = jnp.broadcast_to(jnp.sqrt(total), norm_out.shape)
+        line_a.sent()
+        line_f.sent()
+        sum_f.sent()
+        sum_g.sent()
+        all_early.sent()
+        all_late.sent()
+
     wp_in.sent()
     for copy in wp_cross:
         copy.wait_send()
@@ -642,17 +947,22 @@
     for i, r in enumerate((3, 1, 2)):
         cp(gsend.at[r], gm.at[s], 39 + i, peer(r)).wait_send()
     ga_in.sent()
-    sum_o.sent()
     sum_a.sent()
 
 
-def run_layer(frames, mask_col, cot, seg_q, seg_k, vec, w_attn, w_ffn):
+def run_layer(frames, mask_col, cot, seg_q, seg_k, vec, attn_src, ffn_src, inside, chips):
     rows, width = frames.shape
     group = 4 * rows
-    hidden = w_ffn.shape[1]
     local = width // 4
+    slab_count = 2 * chips if inside else SLABS
+    hidden = ffn_src.shape[0] if inside else ffn_src.shape[1]
+    attn_shape = (slab_count, local, attn_src.shape[-1])
+    ffn_shape = (slab_count, hidden, ffn_src.shape[-1])
     vmem = pl.BlockSpec(memory_space=pltpu.VMEM)
+    anywhere = pl.BlockSpec(memory_space=pl.ANY)
+    source = anywhere if inside else vmem
     block = (4, rows, width)
+    sums = (8, width)
     scratch = [
         pltpu.VMEM(block, BF16),
         pltpu.VMEM(block, BF16),
@@ -665,10 +975,8 @@
         pltpu.VMEM((4, 4, rows, local), BF16),
         pltpu.VMEM(block, BF16),
         pltpu.VMEM((4, rows, hidden), BF16),
-        pltpu.VMEM((4, rows, hidden), BF16),
         pltpu.VMEM((rows, width), F32),
         pltpu.VMEM((rows, width), F32),
-        pltpu.VMEM((3, rows, width), BF16),
         pltpu.VMEM((3, rows, width), BF16),
         pltpu.VMEM((rows, width), BF16),
         pltpu.VMEM((rows, width), BF16),
@@ -686,25 +994,48 @@
         pltpu.VMEM((3, 4, rows, local), BF16),
         pltpu.VMEM((group, LANES), F32),
         pltpu.VMEM((group, LANES), F32),
-        pltpu.SemaphoreType.DMA((60,)),
-        pltpu.SemaphoreType.DMA((60,)),
     ]
+    sem_count = 75 + 14 * chips if inside else 60
+    scratch += [pltpu.SemaphoreType.DMA((sem_count,)), pltpu.SemaphoreType.DMA((sem_count,))]
+    scratch.append(pltpu.SemaphoreType.DMA((4,)))
+    if inside:
+        scratch += [
+            pltpu.VMEM(attn_shape, BF16),
+            pltpu.VMEM(ffn_shape, BF16),
+            pltpu.VMEM(attn_shape, BF16),
+            pltpu.VMEM(ffn_shape, BF16),
+            pltpu.VMEM((chips, *attn_shape[1:]), BF16),
+            pltpu.VMEM((chips, *ffn_shape[1:]), BF16),
+            pltpu.VMEM((chips + 1, *attn_shape[1:]), BF16),
+            pltpu.VMEM((chips + 1, *ffn_shape[1:]), BF16),
+            pltpu.VMEM(sums, F32),
+            pltpu.VMEM(sums, F32),
+            pltpu.VMEM((2, 8, *sums), F32),
+            pltpu.VMEM((2, chips, *sums), F32),
+        ]
+        last = (
+            jax.ShapeDtypeStruct(vec.shape, F32),
+            jax.ShapeDtypeStruct((8, LANES), F32),
+            jax.ShapeDtypeStruct(attn_shape[1:], F32),
+            jax.ShapeDtypeStruct(ffn_shape[1:], F32),
+        )
+    else:
+        last = (
+            jax.ShapeDtypeStruct(sums, F32),
+            jax.ShapeDtypeStruct(sums, F32),
+            jax.ShapeDtypeStruct(attn_shape, BF16),
+            jax.ShapeDtypeStruct(ffn_shape, BF16),
+        )
     return pl.pallas_call(
-        layer_kernel,
-        out_shape=(
-            jax.ShapeDtypeStruct((rows, width), BF16),
-            jax.ShapeDtypeStruct((rows, width), F32),
-            jax.ShapeDtypeStruct(vec.shape, F32),
-            jax.ShapeDtypeStruct(w_attn.shape, BF16),
-            jax.ShapeDtypeStruct(w_ffn.shape, BF16),
-        ),
-        in_specs=[vmem] * 8,
-        out_specs=(vmem,) * 5,
+        functools.partial(layer_kernel, inside, chips),
+        out_shape=(jax.ShapeDtypeStruct((rows, width), BF16), jax.ShapeDtypeStruct((rows, width), F32), *last),
+        in_specs=[vmem, vmem, anywhere, vmem, vmem, vmem, source, source],
+        out_specs=(vmem,) * 6,
         scratch_shapes=scratch,
         compiler_params=pltpu.CompilerParams(
-            collective_id=0, has_side_effects=True, vmem_limit_bytes=60 * 1024 * 1024
+            collective_id=0, has_side_effects=True, vmem_limit_bytes=VMEM_LIMIT
         ),
-    )(frames, mask_col, cot, seg_q, seg_k, vec, w_attn, w_ffn)
+    )(frames, mask_col, cot, seg_q, seg_k, vec, attn_src, ffn_src)
 
 
 def per_device(
@@ -727,13 +1058,8 @@
 
     def gather_slabs(master):
         shard = master.astype(BF16)
-        if dp_count == SLABS:
-            return lax.all_gather(shard, "dp", axis=0)
         whole = lax.all_gather(shard, "dp", axis=1, tiled=True)
         return whole.reshape(shard.shape[0], SLABS, -1).transpose(1, 0, 2)
-
-    w_attn = gather_slabs(attn_master)
-    w_ffn = gather_slabs(ffn_master)
 
     positions = lax.iota(jnp.int32, group)
     starts = span_starts[0]
@@ -749,22 +1075,28 @@
         first.astype(F32),
         jnp.where(lane == 1, second.astype(F32), ((lane >= 2) & (lane <= 4)).astype(F32)),
     )
-    output, frames_grad, vec_local, g_attn, g_ffn = run_layer(
-        frames[0], mask_col, cotangent[0], seg_q.astype(BF16), seg_k.astype(BF16), vec_master, w_attn, w_ffn
-    )
-
-    def scatter_slabs(slabs):
-        slabs = slabs.astype(F32)
-        if dp_count == SLABS:
-            return lax.psum_scatter(slabs, "dp", scatter_dimension=0, tiled=False)
-        whole = slabs.transpose(1, 0, 2).reshape(slabs.shape[1], -1)
-        return lax.psum_scatter(whole, "dp", scatter_dimension=1, tiled=True)
-
-    attn_owned = scatter_slabs(g_attn)
-    ffn_owned = scatter_slabs(g_ffn)
-    owned_squares = jnp.sum(attn_owned * attn_owned) + jnp.sum(ffn_owned * ffn_owned)
-    vec_grad, total_squares = lax.psum((vec_local, owned_squares), ("seq", "dp"))
-    grad_norm = jnp.sqrt(total_squares + jnp.sum(vec_grad * vec_grad))
+    inside = attn_master.shape[1] % 256 == 0 and ffn_master.shape[1] % 256 == 0 and dp_count in (4, 8)
+    head = (frames[0], mask_col, cotangent[0], seg_q.astype(BF16), seg_k.astype(BF16), vec_master)
+    if inside:
+        output, frames_grad, vec_grad, norm, attn_owned, ffn_owned = run_layer(
+            *head, attn_master, ffn_master, True, dp_count // 2
+        )
+        grad_norm = norm[0, 0]
+    else:
+        output, frames_grad, early, late, g_attn, g_ffn = run_layer(
+            *head, gather_slabs(attn_master), gather_slabs(ffn_master), False, dp_count // 2
+        )
+        vec_local = jnp.concatenate([late[0:4], early[0:4], late[4:5], early[4:8]], axis=0)
+
+        def scatter_slabs(slabs):
+            whole = slabs.astype(F32).transpose(1, 0, 2).reshape(slabs.shape[1], -1)
+            return lax.psum_scatter(whole, "dp", scatter_dimension=1, tiled=True)
+
+        attn_owned = scatter_slabs(g_attn)
+        ffn_owned = scatter_slabs(g_ffn)
+        owned_squares = jnp.sum(attn_owned * attn_owned) + jnp.sum(ffn_owned * ffn_owned)
+        vec_grad, total_squares = lax.psum((vec_local, owned_squares), ("seq", "dp"))
+        grad_norm = jnp.sqrt(total_squares + jnp.sum(vec_grad * vec_grad))
     clip = jnp.minimum(1.0, MAX_NORM / (grad_norm + 1e-06))
     attn_new, attn_first_new, attn_second_new = adam_step(
         attn_master, attn_first, attn_second, attn_owned * clip, RATE_ATTN, DECAY_RATE

time: 457 us -> 232 us (0.51)
  waiting for transfers between devices: 204 us -> 0 us
  Pallas kernels: 164 us -> 217 us
  blocking collectives: 38.7 us -> 0 us
  other arithmetic: 28.7 us -> 8.66 us
  between operations: 17.7 us -> 1.5 us
    reduce_scatter x2 -> x0, waiting for transfers between devices: 130 us -> none  [scatter_slabs(): return lax.psum_scatter(slabs, 'dp', scatter_dimension=0, tiled=False)]
    all_gather x2 -> x0, waiting for transfers between devices: 74.4 us -> none  [gather_slabs(): return lax.all_gather(shard, 'dp', axis=0)]
    pallas_call x1, Pallas kernels: 164 us -> 217 us  [run_layer(): pl.pallas_call(functools.partial(layer_kernel, inside, chips), out_shape=...]
    psum x1 -> x0, blocking collectives: 38.7 us -> none  [per_device(): lax.psum((vec_local, owned_squares), ('seq', 'dp'))]
    convert_element_type x4 -> x0, other arithmetic: 14.1 us -> none  [the longest x2 10.2 us: scatter_slabs(): slabs = slabs.astype(F32)]
    reduce_sum x3 -> x0, other arithmetic: 4.58 us -> none  [the longest x1 2.19 us: per_device(): jnp.sum(ffn_owned * ffn_owned)]
  transfers between devices with their start and end apart: 4 -> 0, of which waited for: 4 -> 0; matrix products, arithmetic and copies ran while one was open for 3% -> 0% of each run, Pallas kernels for 0% -> 0%
where the time goes in v2:
time: 232 us
  Pallas kernels  217 us (94%)
  other arithmetic  8.66 us (4%)
  local copies, waits for them, and re-layouts  5.38 us (2%)
    pallas_call x1, Pallas kernels, run_layer(): pl.pallas_call(functools.partial(layer_kernel, inside, chips), out_shape=...  217 us

profile of v2, /device:TPU:0, one launch (start us, length us, event | category | flops | bytes accessed | tf_op | source)
XLA Modules:
  0.0 232.2 jit_solution(2595164131608495635)
XLA Ops:
  0.6 0.0 copy-start.13
  0.7 0.6 copy-done.13
  1.3 0.1 fusion.3
  1.4 1.0 copy.28.refs_1_
  2.5 0.7 copy-done.12
  3.2 1.4 select_convert_fusion
  4.6 216.6 %shard_map.236 = (bf16[256,1024]{1,0:T(8,128)(2,1)}, f32[256,1024]{1,0:T(8,128)}, f32[13,1024]{1,0:T(8,128)}, f32[8,128]{1,0:T(8,128)}, f32[256,512]{1,0:T(8,128)}, /*index=5*/f32[1024,256]{1,0:T(8,128)}) custom-call(bf16[256,1024]{1,0:T(8,128)(2,1)} %bitcast.14, f32[1024,1]{1,0:T(8,128)} %copy.28.refs_1_, bf16[256,1024]{1,0:T(8,128)(2,1)} %bitcast.15, ...), custom_call_target="tpu_custom_call" | custom-call | tf_op jit(solution)/shard_map/pallas_call | solution.py:1029
  221.3 1.2 slice.3
  223.1 0.0 copy-done.1
  223.2 0.0 copy-done.5
  223.2 0.0 copy-done.6
  223.2 0.0 copy-start
  223.2 0.0 copy-start.2
  223.2 0.0 copy-start.3
  223.2 2.7 %fusion.8 = (bf16[256,512]{1,0:T(8,128)(2,1)}, f32[256,512]{1,0:T(8,128)}, f32[256,512]{1,0:T(8,128)}, f32[256,512]{1,0:T(8,128)}) fusion(f32[256,512]{1,0:T(8,128)S(1)} %copy-done.1, f32[256,512]{1,0:T(8,128)} %get-tuple-element.23, f32[]{:T(128)S(6)} %min.3, f32[256,512]{1,0:T(8,128)S(1)} %copy-done.5, f32[256,512]{1,0:T(8,128)S(1)} %copy-done.6), kind=kLoop, calls=%fused_computation.27 | loop fusion | flops 2228224 | bytes 3932164 | tf_op jit(solution)/shard_map/convert_element_type | solution.py:1117
  225.9 0.0 copy-done.2
  225.9 0.0 copy-start.8
  225.9 0.0 copy-start.9
  226.0 0.0 copy-start.10
  226.0 3.7 %fusion.6 = (bf16[1024,256]{1,0:T(8,128)(2,1)}, f32[1024,256]{1,0:T(8,128)}, f32[1024,256]{1,0:T(8,128)}, f32[1024,256]{1,0:T(8,128)}) fusion(f32[1024,256]{1,0:T(8,128)S(1)} %copy-done, f32[1024,256]{1,0:T(8,128)} %get-tuple-element.24, f32[]{:T(128)S(6)} %min.3, f32[1024,256]{1,0:T(8,128)S(1)} %copy-done.2, f32[1024,256]{1,0:T(8,128)S(1)} %copy-done.3), kind=kLoop, calls=%fused_computation.26 | loop fusion | flops 4456448 | bytes 7864324 | tf_op jit(solution)/shard_map/convert_element_type | solution.py:1121
  229.7 0.0 copy-done.10
  229.7 0.7 multiply_subtract_fusion.2
  230.4 0.8 copy.31
  231.2 1.0 copy.32
  (20 shorter events, 0.1 us)
Async XLA Ops:
  0.6 0.7 copy-start.13
  2.5 0.7 copy-start.12
  4.6 218.5 %copy-start.1 = (f32[256,512]{1,0:T(8,128)S(1)}, f32[256,512]{1,0:T(8,128)}, u32[]{:S(2)}) copy-start(f32[256,512]{1,0:T(8,128)} %refs_6_.1) | copy-start | bytes 1572868
  4.6 218.6 %copy-start.5 = (f32[256,512]{1,0:T(8,128)S(1)}, f32[256,512]{1,0:T(8,128)}, u32[]{:S(2)}) copy-start(f32[256,512]{1,0:T(8,128)} %param.18) | copy-start | bytes 1572868
  4.6 218.6 %copy-start.6 = (f32[256,512]{1,0:T(8,128)S(1)}, f32[256,512]{1,0:T(8,128)}, u32[]{:S(2)}) copy-start(f32[256,512]{1,0:T(8,128)} %param.19) | copy-start | bytes 1572868
  223.2 2.7 %copy-start = (f32[1024,256]{1,0:T(8,128)S(1)}, f32[1024,256]{1,0:T(8,128)}, u32[]{:S(2)}) copy-start(f32[1024,256]{1,0:T(8,128)} %refs_7_.1) | copy-start | bytes 3145732
  223.2 2.7 %copy-start.2 = (f32[1024,256]{1,0:T(8,128)S(1)}, f32[1024,256]{1,0:T(8,128)}, u32[]{:S(2)}) copy-start(f32[1024,256]{1,0:T(8,128)} %param.21) | copy-start | bytes 3145732
  223.2 2.7 %copy-start.3 = (f32[1024,256]{1,0:T(8,128)S(1)}, f32[1024,256]{1,0:T(8,128)}, u32[]{:S(2)}) copy-start(f32[1024,256]{1,0:T(8,128)} %param.22) | copy-start | bytes 3145732
  225.9 3.7 %copy-start.8 = (f32[13,1024]{1,0:T(8,128)S(1)}, f32[13,1024]{1,0:T(8,128)}, u32[]{:S(2)}) copy-start(f32[13,1024]{1,0:T(8,128)} %refs_5_.1) | copy-start | bytes 159748
  225.9 3.7 %copy-start.9 = (f32[13,1024]{1,0:T(8,128)S(1)}, f32[13,1024]{1,0:T(8,128)}, u32[]{:S(2)}) copy-start(f32[13,1024]{1,0:T(8,128)} %param.24) | copy-start | bytes 159748
  226.0 3.7 %copy-start.10 = (f32[13,1024]{1,0:T(8,128)S(1)}, f32[13,1024]{1,0:T(8,128)}, u32[]{:S(2)}) copy-start(f32[13,1024]{1,0:T(8,128)} %param.25) | copy-start | bytes 159748
  226.0 3.7 %copy-start.11 = (f32[13,1024]{1,0:T(8,128)S(1)}, f32[13,1024]{1,0:T(8,128)}, u32[]{:S(2)}) copy-start(f32[13,1024]{1,0:T(8,128)} %get-tuple-element.25) | copy-start | bytes 159748
  226.0 4.4 %copy-start.7 = (bf16[256,1024]{1,0:T(8,128)(2,1)S(1)}, bf16[256,1024]{1,0:T(8,128)(2,1)}, u32[]{:S(2)}) copy-start(bf16[256,1024]{1,0:T(8,128)(2,1)} %get-tuple-element.20) | copy-start | bytes 1572868
  229.7 1.5 copy-start.4

commit v3 on v2

--- a/solution.py
+++ b/solution.py
@@ -125,31 +125,29 @@
 class Scatter:
     def __init__(self, cp, part, in_x, in_y, via_x, via_y, base, place):
         _, px, py, _ = place
-        h = in_x.shape[0] // 2
+        h = in_x.shape[1] // 2
         top, bot = pl.ds(0, h), pl.ds(h, h)
-        self.part, self.via_x, self.via_y, self.h = part, via_x, via_y, h
+        self.to_x, self.to_y, self.via_x, self.via_y = part(1), part(2), via_x, via_y
+        self.top, self.bot = top, bot
+        far = part(3)
         self.copies = [
-            cp(part.at[2, top], via_x, base, px),
-            cp(part.at[2, bot], via_y, base + 1, py),
-            cp(part.at[0, top], in_x.at[top], base + 2, px),
-            cp(part.at[1, bot], in_y.at[bot], base + 3, py),
-            cp(part.at[1, top], in_y.at[top], base + 4, py),
-            cp(part.at[0, bot], in_x.at[bot], base + 5, px),
+            cp(far.at[:, top], via_x, base, px),
+            cp(far.at[:, bot], via_y, base + 1, py),
+            cp(self.to_x.at[:, top], in_x.at[:, top], base + 2, px),
+            cp(self.to_y.at[:, bot], in_y.at[:, bot], base + 3, py),
+            cp(self.to_y.at[:, top], in_y.at[:, top], base + 4, py),
+            cp(self.to_x.at[:, bot], in_x.at[:, bot], base + 5, px),
         ]
 
     def start(self, relation):
         for i in {3: (0, 1), 1: (2,), 2: (3,)}[relation]:
             self.copies[i].start()
 
-    def relay_y(self):
-        self.copies[0].wait_recv()
-        self.part[1, : self.h, :] = (self.part[1, : self.h, :].astype(F32) + self.via_x[...].astype(F32)).astype(BF16)
-        self.copies[4].start()
-
-    def relay_x(self):
-        self.copies[1].wait_recv()
-        self.part[0, self.h :, :] = (self.part[0, self.h :, :].astype(F32) + self.via_y[...].astype(F32)).astype(BF16)
-        self.copies[5].start()
+    def relay(self):
+        for i, ref, via, at in ((0, self.to_y, self.via_x, self.top), (1, self.to_x, self.via_y, self.bot)):
+            self.copies[i].wait_recv()
+            ref[:, at, :] = (ref[:, at, :].astype(F32) + via[...].astype(F32)).astype(BF16)
+            self.copies[4 + i].start()
 
     def wait(self):
         for i in (2, 3, 4, 5):
@@ -389,7 +387,7 @@
         del refs[:count]
         return head
 
-    frames, mask_col, cot, seg_q, seg_k, vec, attn_src, ffn_src = take(8)
+    frames, segments, spans, cot, vec, attn_src, ffn_src = take(7)
     if inside:
         out, frames_grad, vec_out, norm_out, attn_owned, ffn_owned = take(6)
     else:
@@ -398,9 +396,11 @@
     fr_g, cot_g, a_g, wp, qa, ka, va, kt, att, b_g, gp_g = take(11)
     act_g = fr_g
     resid, own, part, in_x, in_y, via_x, via_y, in_x2, in_y2, via_x2, via_y2 = take(11)
-    gsend, gm, dom, ga_g, gres, dqkv, dk_acc, dv_acc, send_sem, recv_sem, local_sem = take(11)
-    if inside:
-        w_attn, w_ffn, g_attn, g_ffn, cross_a, cross_f, landed_a, landed_f, early, late, planes, lines = take(12)
+    gsend, gm, dom, ga_g, gres, dqkv, dk_acc, dv_acc, mask_col, seg_q, seg_k = take(11)
+    send_sem, recv_sem, local_sem = take(3)
+    if inside:
+        w_attn, w_ffn, g_attn, g_ffn, cross_a, cross_f, landed_a, landed_f = take(8)
+        early, late, squares, planes, lines, planes_s, lines_s = take(7)
     s = lax.axis_index("seq")
     d = lax.axis_index("dp")
     core = lax.rem(d, 2)
@@ -451,7 +451,8 @@
     per_a = width // slab_a
     per_f = width // slab_f
     tile = 256
-    chunk = 32
+    chunk = 128
+    small = 64
 
     cot_load = pltpu.make_async_copy(cot, cot_g.at[s], local_sem.at[0])
     cot_load.start()
@@ -501,6 +502,18 @@
     ]
     early[...] = jnp.zeros_like(early)
     late[...] = jnp.zeros_like(late)
+
+    group = 4 * rows
+    position = lax.broadcasted_iota(jnp.int32, (group, spans.shape[1]), 0)
+    starts = spans[...]
+    covered = jnp.logical_and(position >= starts, position < starts + SPAN)
+    mask_col[...] = jnp.max(jnp.where(covered, 1.0, 0.0), axis=1, keepdims=True)
+    second = jnp.transpose(jnp.broadcast_to(segments[...].astype(F32), (LANES, group)))
+    seg_lane = lax.broadcasted_iota(jnp.int32, (group, LANES), 1)
+    fill = jnp.where(seg_lane == 0, second, jnp.where(seg_lane == 1, 1.0 - second, 0.0)) * NEG_FILL
+    seg_q[...] = fill.astype(BF16)
+    ones = jnp.where(seg_lane < 5, 1.0, 0.0)
+    seg_k[...] = jnp.where(seg_lane == 0, 1.0 - second, jnp.where(seg_lane == 1, second, ones)).astype(BF16)
     half = rows // 2
 
     lane = lax.broadcasted_iota(jnp.int32, (rows, LANES), 1)
@@ -568,7 +581,6 @@
     lax.fori_loop(0, 4, lambda j, carry: (project_in(j), carry)[1], 0)
     wp_in.relay()
     cot_load.wait()
-    cot_in.start()
 
     def att_x(j, slot):
         return cp(att.at[slot, j], att.at[slot, j], 21 + j, px)
@@ -626,17 +638,18 @@
 
         return carry
 
-    lax.fori_loop(0, 3, attend, 0)
-    ffn_step(1)
-    lax.fori_loop(3, 4, attend, 0)
-    att_relay(3, True)
+    lax.fori_loop(0, 2, attend, 0)
     wp_in.wait_x()
     wp_cross[0].start()
     wp_in.wait_y()
     wp_cross[1].start()
     wp_in.wait_d()
     wp_cross[2].start()
-    cot_in.relay()
+    lax.fori_loop(2, 3, attend, 0)
+    ffn_step(1)
+    lax.fori_loop(3, 4, attend, 0)
+    att_relay(3, True)
+    cot_in.start()
     other_off = pl.multiple_of((1 - core) * half, half)
     for i, p in enumerate((px, py, pd)):
         cp_sib(wp.at[p, pl.ds(other_off, half)], wp.at[p, pl.ds(other_off, half)], 12 + i).wait_recv()
@@ -676,13 +689,15 @@
         lax.fori_loop(0, rows // chunk, norm_rows, 0)
         return carry
 
-    lax.fori_loop(0, 3, project, 0)
+    lax.fori_loop(0, 2, project, 0)
     ffn_step(2)
-    lax.fori_loop(3, 4, project, 0)
+    lax.fori_loop(2, 4, project, 0)
+    cot_in.relay()
     ffn_step(3)
     if inside:
         for shard in range(chips):
             line_f.crossed(shard)
+    frames_in.sent()
 
     def feed(r):
         blk = peer(r)
@@ -709,27 +724,54 @@
             if r == 0:
                 own[:, at] = value
             else:
-                part[r - 1, :, at] = value.astype(BF16)
-
-    sum_b = Scatter(cp, part, in_x, in_y, via_x, via_y, 33, place)
+                part[r - 1, k] = value.astype(BF16)
+
+    sum_b = Scatter(cp, lambda r: part.at[r - 1], in_x, in_y, via_x, via_y, 33, place)
+    feed(0)
     cot_in.wait_x()
+    feed(1)
+    sum_b.start(1)
     cot_in.wait_y()
+    feed(2)
+    sum_b.start(2)
     cot_in.wait_d()
-    frames_in.sent()
     feed(3)
     sum_b.start(3)
-    feed(1)
-    sum_b.start(1)
-    feed(2)
-    sum_b.start(2)
-    sum_b.relay_y()
-    sum_b.relay_x()
-    feed(0)
+
+    def ffn_grads(i, carry):
+        at = pl.ds(pl.multiple_of(i * tile, tile), tile)
+        for left, right, first in ((gp_g, b_g, 0), (act_g, cot_g, per_f)):
+            turned = jnp.transpose(jnp.concatenate([left[p, :, at] for p in range(4)], axis=0))
+            for k in range(per_f):
+                cols = jnp.concatenate([right[p, :, k * slab_f : (k + 1) * slab_f] for p in range(4)], axis=0)
+                g_ffn[first + k, at, :] = nn(turned, cols).astype(BF16)
+        return carry
+
+    lax.fori_loop(0, w_ffn.shape[1] // tile, ffn_grads, 0)
+    sum_step = no_step
+    if inside:
+        sum_f = LineSum(cp_dp, g_ffn, cross_f, landed_f, 60 + 6 * chips, chip, core, chips)
+        sum_g = LineSum(cp_dp, g_attn, cross_a, landed_a, 60 + 9 * chips, chip, core, chips)
+        all_early = Everyone(cp_any, planes.at[0], lines.at[0], 60 + 12 * chips, s, chip, core, chips)
+        all_late = Everyone(cp_any, planes.at[1], lines.at[1], 67 + 13 * chips, s, chip, core, chips)
+        all_squares = Everyone(cp_any, planes_s, lines_s, 74 + 14 * chips, s, chip, core, chips)
+        sum_step = sum_f.step
+        for shard in range(chips):
+            sum_f.start(shard)
+    sum_b.relay()
+    if inside:
+        for shard in range(chips):
+            sum_f.fold(shard)
+    sum_step(0)
     sum_b.wait()
 
+    def landed(from_x, from_y, at):
+        tiles = range(from_x.shape[0])
+        return jnp.concatenate([from_x[t, at, :].astype(F32) + from_y[t, at, :].astype(F32) for t in tiles], axis=1)
+
     def back_two(i, carry):
-        at = pl.ds(pl.multiple_of(i * chunk, chunk), chunk)
-        grad_b = own[at, :] + in_x[at, :].astype(F32) + in_y[at, :].astype(F32)
+        at = pl.ds(pl.multiple_of(i * small, small), small)
+        grad_b = own[at, :] + landed(in_x, in_y, at)
         normed, inv_std = normalise(resid[at, :])
         grad_y = cot_g[s, at, :].astype(F32)
         grad_resid = grad_y + norm_back(grad_b, normed, inv_std, vec[5:6, :])
@@ -742,7 +784,7 @@
         early[3:4, :] += col_sum(grad_y)
         return carry
 
-    lax.fori_loop(0, rows // chunk, back_two, 0)
+    lax.fori_loop(0, rows // small, back_two, 0)
 
     for i, r in enumerate((3, 1, 2)):
         gsend[r] = nt(ga_g[s], wp[peer(r)]).astype(BF16)
@@ -751,37 +793,20 @@
     ga_in = Gather(cp, ga_g, 42, place, 0, rows)
     ga_in.start()
     sum_b.sent()
-
-    sum_o = Scatter(cp, part, in_x2, in_y2, via_x2, via_y2, 48, place)
+    if inside:
+        all_early.start(early[...])
 
     def out_part(blk, k):
         return nn(act_g[blk], w_ffn[per_f + k])
 
+    for j in range(4):
+        att_x(j, s).wait_send()
+        att_y(j, s).wait_send()
+        att_relay(j, False)
+    sum_o = Scatter(cp, lambda r: att.at[peer(r)], in_x2, in_y2, via_x2, via_y2, 48, place)
     for r in (3, 1, 2):
         for k in range(per_f):
-            part[r - 1, :, k * slab_f : (k + 1) * slab_f] = out_part(peer(r), k).astype(BF16)
-        sum_o.start(r)
-
-    def ffn_grads(i, carry):
-        at = pl.ds(pl.multiple_of(i * tile, tile), tile)
-        for left, right, first in ((gp_g, b_g, 0), (act_g, cot_g, per_f)):
-            turned = jnp.transpose(jnp.concatenate([left[p, :, at] for p in range(4)], axis=0))
-            for k in range(per_f):
-                cols = jnp.concatenate([right[p, :, k * slab_f : (k + 1) * slab_f] for p in range(4)], axis=0)
-                g_ffn[first + k, at, :] = nn(turned, cols).astype(BF16)
-        return carry
-
-    lax.fori_loop(0, w_ffn.shape[1] // tile, ffn_grads, 0)
-    sum_step = no_step
-    if inside:
-        sum_f = LineSum(cp_dp, g_ffn, cross_f, landed_f, 60 + 6 * chips, chip, core, chips)
-        sum_g = LineSum(cp_dp, g_attn, cross_a, landed_a, 60 + 9 * chips, chip, core, chips)
-        all_early = Everyone(cp_any, planes.at[0], lines.at[0], 60 + 12 * chips, s, chip, core, chips)
-        all_late = Everyone(cp_any, planes.at[1], lines.at[1], 67 + 13 * chips, s, chip, core, chips)
-        sum_step = sum_f.step
-        for shard in range(chips):
-            sum_f.start(shard)
-        all_early.start(early[...])
+            att[peer(r), k] = out_part(peer(r), k).astype(BF16)
 
     for i, r in enumerate((3, 1, 2)):
         cp(gsend.at[r], gm.at[peer(r)], 39 + i, peer(r)).wait_recv()
@@ -794,17 +819,8 @@
         return carry
 
     lax.fori_loop(0, 4, spread, 0)
-    if inside:
-        for shard in range(chips):
-            sum_f.fold(shard)
-    sum_step(0)
-    ga_in.relay()
-    sum_o.relay_y()
-    sum_o.relay_x()
-    if inside:
-        all_early.middle()
-
-    def back_pair(pair):
+
+    def back_pair(pair, between):
         dk_acc[...] = jnp.zeros_like(dk_acc)
         dv_acc[...] = jnp.zeros_like(dv_acc)
 
@@ -824,19 +840,19 @@
             dqkv[0, j, :, pair * LANES : (pair + 1) * LANES] = (jnp.transpose(turned) * 0.125).astype(BF16)
             return carry
 
-        lax.fori_loop(0, 4, back_block, 0)
+        lax.fori_loop(0, 2, back_block, 0)
+        between()
+        lax.fori_loop(2, 4, back_block, 0)
         for j in range(4):
             at = slice(j * rows, (j + 1) * rows)
             dqkv[1, j, :, pair * LANES : (pair + 1) * LANES] = dk_acc[at, :].astype(BF16)
             dqkv[2, j, :, pair * LANES : (pair + 1) * LANES] = dv_acc[at, :].astype(BF16)
 
-    back_pair(0)
+    back_pair(0, ga_in.relay)
     sum_step(1)
-    back_pair(1)
-    sum_step(2)
-
-    sum_o.sent()
-    sum_a = Scatter(cp, part, in_x, in_y, via_x, via_y, 54, place)
+    back_pair(1, all_early.middle if inside else lambda: None)
+
+    sum_a = Scatter(cp, lambda r: part.at[r - 1], in_x, in_y, via_x, via_y, 54, place)
 
     def grad_in(r):
         blk = peer(r)
@@ -848,13 +864,9 @@
             if r == 0:
                 own[:, at] = value
             else:
-                part[r - 1, :, at] = value.astype(BF16)
-
-    sum_o.wait()
-    for k in range(per_f):
-        at = slice(k * slab_f, (k + 1) * slab_f)
-        total = out_part(s, k) + resid[:, at] + in_x2[:, at].astype(F32) + in_y2[:, at].astype(F32) + vec[7:8, at]
-        out[:, at] = total.astype(BF16)
+                per_tile = slab_a // tile
+                for t in range(per_tile):
+                    part[r - 1, k * per_tile + t] = value[:, t * tile : (t + 1) * tile].astype(BF16)
 
     for r in (3, 1, 2):
         grad_in(r)
@@ -874,8 +886,6 @@
 
     attn_grads(0)
     attn_grads(1)
-    sum_a.relay_y()
-    sum_a.relay_x()
     attn_grads(2)
     ga_in.wait_x()
     ga_in.wait_y()
@@ -888,16 +898,20 @@
     if inside:
         for shard in range(chips):
             sum_g.start(shard)
-        sum_f.finish(ffn_owned)
+    sum_a.relay()
+    for r in (3, 1, 2):
+        sum_o.start(r)
+    sum_step(2)
+    if inside:
         for shard in range(chips):
             sum_g.fold(shard)
         sum_g.step(0)
     sum_a.wait()
 
     def back_one(i, carry):
-        at = pl.ds(pl.multiple_of(i * chunk, chunk), chunk)
-        at_all = pl.ds(pl.multiple_of(s * rows + i * chunk, chunk), chunk)
-        grad_a = own[at, :] + in_x[at, :].astype(F32) + in_y[at, :].astype(F32)
+        at = pl.ds(pl.multiple_of(i * small, small), small)
+        at_all = pl.ds(pl.multiple_of(s * rows + i * small, small), small)
+        grad_a = own[at, :] + landed(in_x, in_y, at)
         masked = mask_col[at_all, :] > 0.0
         normed, inv_std = normalise(jnp.where(masked, vec[8:9, :], frames[at, :].astype(F32)))
         grad_x = gres[at, :] + norm_back(grad_a, normed, inv_std, vec[0:1, :])
@@ -907,23 +921,40 @@
         late[4:5, :] += col_sum(jnp.where(masked, grad_x, 0.0))
         return carry
 
-    lax.fori_loop(0, rows // chunk, back_one, 0)
-    if inside:
+    lax.fori_loop(0, rows // small, back_one, 0)
+    if inside:
+        all_late.start(late[...])
+        sum_f.finish(ffn_owned)
+        squares[...] = jnp.zeros_like(squares)
+        ffn_squares = col_sum(ffn_owned[...] * ffn_owned[...])
         sum_g.step(1)
+    sum_o.relay()
+    if inside:
+        all_late.middle()
         sum_g.step(2)
-        sum_g.finish(attn_owned)
-        late[5:6, :slab_a] = col_sum(attn_owned[...] * attn_owned[...])
-        late[5:6, slab_a : slab_a + slab_f] = col_sum(ffn_owned[...] * ffn_owned[...])
-        all_late.start(late[...])
+    sum_o.wait()
+    for k in range(per_f):
+        at = slice(k * slab_f, (k + 1) * slab_f)
+        total = out_part(s, k) + resid[:, at] + in_x2[k].astype(F32) + in_y2[k].astype(F32) + vec[7:8, at]
+        out[:, at] = total.astype(BF16)
+
+    if inside:
         whole_early = all_early.end()
-        all_late.middle()
         whole_late = all_late.end()
         vec_out[0:4, :] = whole_late[0:4]
         vec_out[4:8, :] = whole_early[0:4]
         vec_out[8:9, :] = whole_late[4:5]
         vec_out[9:13, :] = whole_early[4:8]
-        vec_square = vec_out[...] * vec_out[...]
-        total = jnp.sum(col_sum(vec_square) + whole_late[5:6], axis=1, keepdims=True)
+        vec_square = col_sum(vec_out[...] * vec_out[...])
+        sum_g.finish(attn_owned)
+        attn_squares = col_sum(attn_owned[...] * attn_owned[...])
+        owned_squares = sum(attn_squares[:, i * LANES : (i + 1) * LANES] for i in range(slab_a // LANES))
+        owned_squares += sum(ffn_squares[:, i * LANES : (i + 1) * LANES] for i in range(slab_f // LANES))
+        squares[0:1, :] = owned_squares
+        all_squares.start(squares[...])
+        all_squares.middle()
+        whole_squares = all_squares.end()
+        total = jnp.sum(whole_squares[0:1], axis=1, keepdims=True) + jnp.sum(vec_square, axis=1, keepdims=True)
         norm_out[...] = jnp.broadcast_to(jnp.sqrt(total), norm_out.shape)
         line_a.sent()
         line_f.sent()
@@ -931,26 +962,21 @@
         sum_g.sent()
         all_early.sent()
         all_late.sent()
+        all_squares.sent()
 
     wp_in.sent()
     for copy in wp_cross:
         copy.wait_send()
     cot_in.sent()
 
-    def att_sent(j, carry):
-        att_x(j, s).wait_send()
-        att_y(j, s).wait_send()
-        att_relay(j, False)
-        return carry
-
-    lax.fori_loop(0, 4, att_sent, 0)
     for i, r in enumerate((3, 1, 2)):
         cp(gsend.at[r], gm.at[s], 39 + i, peer(r)).wait_send()
     ga_in.sent()
     sum_a.sent()
-
-
-def run_layer(frames, mask_col, cot, seg_q, seg_k, vec, attn_src, ffn_src, inside, chips):
+    sum_o.sent()
+
+
+def run_layer(frames, segments, spans, cot, vec, attn_src, ffn_src, inside, chips):
     rows, width = frames.shape
     group = 4 * rows
     local = width // 4
@@ -977,15 +1003,15 @@
         pltpu.VMEM((4, rows, hidden), BF16),
         pltpu.VMEM((rows, width), F32),
         pltpu.VMEM((rows, width), F32),
-        pltpu.VMEM((3, rows, width), BF16),
-        pltpu.VMEM((rows, width), BF16),
-        pltpu.VMEM((rows, width), BF16),
-        pltpu.VMEM((rows // 2, width), BF16),
-        pltpu.VMEM((rows // 2, width), BF16),
-        pltpu.VMEM((rows, width), BF16),
-        pltpu.VMEM((rows, width), BF16),
-        pltpu.VMEM((rows // 2, width), BF16),
-        pltpu.VMEM((rows // 2, width), BF16),
+        pltpu.VMEM((3, 4, rows, local), BF16),
+        pltpu.VMEM((4, rows, local), BF16),
+        pltpu.VMEM((4, rows, local), BF16),
+        pltpu.VMEM((4, rows // 2, local), BF16),
+        pltpu.VMEM((4, rows // 2, local), BF16),
+        pltpu.VMEM((4, rows, local), BF16),
+        pltpu.VMEM((4, rows, local), BF16),
+        pltpu.VMEM((4, rows // 2, local), BF16),
+        pltpu.VMEM((4, rows // 2, local), BF16),
         pltpu.VMEM((4, rows, local), BF16),
         pltpu.VMEM((4, rows, local), BF16),
         pltpu.VMEM((4, 4, rows, LANES), BF16),
@@ -994,8 +1020,11 @@
         pltpu.VMEM((3, 4, rows, local), BF16),
         pltpu.VMEM((group, LANES), F32),
         pltpu.VMEM((group, LANES), F32),
+        pltpu.VMEM((group, 1), F32),
+        pltpu.VMEM((group, LANES), BF16),
+        pltpu.VMEM((group, LANES), BF16),
     ]
-    sem_count = 75 + 14 * chips if inside else 60
+    sem_count = 82 + 15 * chips if inside else 60
     scratch += [pltpu.SemaphoreType.DMA((sem_count,)), pltpu.SemaphoreType.DMA((sem_count,))]
     scratch.append(pltpu.SemaphoreType.DMA((4,)))
     if inside:
@@ -1010,8 +1039,11 @@
             pltpu.VMEM((chips + 1, *ffn_shape[1:]), BF16),
             pltpu.VMEM(sums, F32),
             pltpu.VMEM(sums, F32),
+            pltpu.VMEM((8, LANES), F32),
             pltpu.VMEM((2, 8, *sums), F32),
             pltpu.VMEM((2, chips, *sums), F32),
+            pltpu.VMEM((8, 8, LANES), F32),
+            pltpu.VMEM((chips, 8, LANES), F32),
         ]
         last = (
             jax.ShapeDtypeStruct(vec.shape, F32),
@@ -1029,13 +1061,62 @@
     return pl.pallas_call(
         functools.partial(layer_kernel, inside, chips),
         out_shape=(jax.ShapeDtypeStruct((rows, width), BF16), jax.ShapeDtypeStruct((rows, width), F32), *last),
-        in_specs=[vmem, vmem, anywhere, vmem, vmem, vmem, source, source],
+        in_specs=[vmem, vmem, vmem, anywhere, vmem, source, source],
         out_specs=(vmem,) * 6,
         scratch_shapes=scratch,
         compiler_params=pltpu.CompilerParams(
             collective_id=0, has_side_effects=True, vmem_limit_bytes=VMEM_LIMIT
         ),
-    )(frames, mask_col, cot, seg_q, seg_k, vec, attn_src, ffn_src)
+    )(frames, segments, spans, cot, vec, attn_src, ffn_src)
+
+
+def adam_kernel(norm, *refs):
+    clip = jnp.minimum(1.0, MAX_NORM / (norm[0, 0] + 1e-06))
+    attn, ffn, vec = refs[0:4], refs[4:8], refs[8:12]
+    attn_to, ffn_to, vec_to, norm_to = refs[12:16], refs[16:20], refs[20:23], refs[23]
+
+    def update(source, target, rate, decay):
+        master, first, second, grad = (ref[...] for ref in source)
+        for ref, value in zip(target, adam_step(master, first, second, grad * clip, rate, decay)):
+            ref[...] = value
+        if len(target) > 3:
+            target[3][...] = target[0][...].astype(BF16)
+
+    update(attn, attn_to, RATE_ATTN, DECAY_RATE)
+    update(ffn, ffn_to, RATE_FFN, DECAY_RATE)
+
+    @pl.when(pl.program_id(0) == 0)
+    def _():
+        update(vec, vec_to, RATE_VEC, 0.0)
+        norm_to[0, 0] = norm[0, 0]
+
+
+def run_adam(norm, attn, ffn, vec):
+    steps = 4
+
+    def split(array):
+        return pl.BlockSpec((array.shape[0] // steps, array.shape[1]), lambda i: (i, 0))
+
+    whole = pl.BlockSpec(vec[0].shape, lambda i: (0, 0))
+    scalar = pl.BlockSpec(memory_space=pltpu.SMEM)
+
+    def shapes(array, copy):
+        types = (F32, F32, F32, BF16) if copy else (F32, F32, F32)
+        return tuple(jax.ShapeDtypeStruct(array.shape, t) for t in types)
+
+    return pl.pallas_call(
+        adam_kernel,
+        grid=(steps,),
+        out_shape=(
+            *shapes(attn[0], True),
+            *shapes(ffn[0], True),
+            *shapes(vec[0], False),
+            jax.ShapeDtypeStruct((1, 1), F32),
+        ),
+        in_specs=[scalar] + [split(attn[0])] * 4 + [split(ffn[0])] * 4 + [whole] * 4,
+        out_specs=(*[split(attn[0])] * 4, *[split(ffn[0])] * 4, *[whole] * 3, scalar),
+        compiler_params=pltpu.CompilerParams(vmem_limit_bytes=VMEM_LIMIT),
+    )(norm, *attn, *ffn, *vec)
 
 
 def per_device(
@@ -1054,34 +1135,18 @@
     vec_second,
 ):
     dp_count = lax.axis_size("dp")
-    group = segment_ids.shape[1]
 
     def gather_slabs(master):
         shard = master.astype(BF16)
         whole = lax.all_gather(shard, "dp", axis=1, tiled=True)
         return whole.reshape(shard.shape[0], SLABS, -1).transpose(1, 0, 2)
 
-    positions = lax.iota(jnp.int32, group)
-    starts = span_starts[0]
-    inside = (positions[:, None] >= starts[None, :]) & (positions[:, None] < starts[None, :] + SPAN)
-    mask_col = jnp.any(inside, axis=1).astype(F32)[:, None]
-    seg = segment_ids[0][:, None]
-    lane = lax.broadcasted_iota(jnp.int32, (group, LANES), 1)
-    first, second = seg == 0, seg == 1
-    zero = jnp.zeros((), F32)
-    seg_q = jnp.where(lane == 0, jnp.where(second, NEG_FILL, zero), jnp.where(lane == 1, jnp.where(first, NEG_FILL, zero), zero))
-    seg_k = jnp.where(
-        lane == 0,
-        first.astype(F32),
-        jnp.where(lane == 1, second.astype(F32), ((lane >= 2) & (lane <= 4)).astype(F32)),
-    )
     inside = attn_master.shape[1] % 256 == 0 and ffn_master.shape[1] % 256 == 0 and dp_count in (4, 8)
-    head = (frames[0], mask_col, cotangent[0], seg_q.astype(BF16), seg_k.astype(BF16), vec_master)
+    head = (frames[0], segment_ids, span_starts, cotangent[0], vec_master)
     if inside:
         output, frames_grad, vec_grad, norm, attn_owned, ffn_owned = run_layer(
             *head, attn_master, ffn_master, True, dp_count // 2
         )
-        grad_norm = norm[0, 0]
     else:
         output, frames_grad, early, late, g_attn, g_ffn = run_layer(
             *head, gather_slabs(attn_master), gather_slabs(ffn_master), False, dp_count // 2
@@ -1096,33 +1161,14 @@
         ffn_owned = scatter_slabs(g_ffn)
         owned_squares = jnp.sum(attn_owned * attn_owned) + jnp.sum(ffn_owned * ffn_owned)
         vec_grad, total_squares = lax.psum((vec_local, owned_squares), ("seq", "dp"))
-        grad_norm = jnp.sqrt(total_squares + jnp.sum(vec_grad * vec_grad))
-    clip = jnp.minimum(1.0, MAX_NORM / (grad_norm + 1e-06))
-    attn_new, attn_first_new, attn_second_new = adam_step(
-        attn_master, attn_first, attn_second, attn_owned * clip, RATE_ATTN, DECAY_RATE
+        norm = jnp.broadcast_to(jnp.sqrt(total_squares + jnp.sum(vec_grad * vec_grad)), (8, LANES))
+    updated = run_adam(
+        norm,
+        (attn_master, attn_first, attn_second, attn_owned),
+        (ffn_master, ffn_first, ffn_second, ffn_owned),
+        (vec_master, vec_first, vec_second, vec_grad),
     )
-    ffn_new, ffn_first_new, ffn_second_new = adam_step(
-        ffn_master, ffn_first, ffn_second, ffn_owned * clip, RATE_FFN, DECAY_RATE
-    )
-    vec_new, vec_first_new, vec_second_new = adam_step(
-        vec_master, vec_first, vec_second, vec_grad * clip, RATE_VEC, 0.0
-    )
-    return (
-        output[None],
-        frames_grad[None],
-        grad_norm,
-        attn_new,
-        attn_first_new,
-        attn_second_new,
-        attn_new.astype(BF16),
-        ffn_new,
-        ffn_first_new,
-        ffn_second_new,
-        ffn_new.astype(BF16),
-        vec_new,
-        vec_first_new,
-        vec_second_new,
-    )
+    return (output[None], frames_grad[None], updated[-1].reshape(()), *updated[:-1])
 
 
 def solution(mesh):

time: 232 us -> 190 us (0.82)
  Pallas kernels: 217 us -> 186 us
  other arithmetic: 8.66 us -> 0 us
  local copies, waits for them, and re-layouts: 5.38 us -> 2.37 us
    pallas_call x1, Pallas kernels: 217 us -> 179 us  [run_layer(): pl.pallas_call(functools.partial(layer_kernel, inside, chips), out_shape=...]
    convert_element_type x6 -> x0, other arithmetic: 7.82 us -> none  [the longest x1 3.69 us: per_device(): ffn_new.astype(BF16)]
    pallas_call x0 -> x1, Pallas kernels: none -> 7.26 us  [run_adam(): pl.pallas_call(adam_kernel, grid=(steps,), out_shape=(*shapes(attn[0], Tr...]
where the time goes in v3:
time: 190 us; the launch traced here: 189 us
  Pallas kernels  186 us (98%)
  local copies, waits for them, and re-layouts  2.37 us (1%)
    pallas_call x1, Pallas kernels, run_layer(): pl.pallas_call(functools.partial(layer_kernel, inside, chips), out_shape=...  179 us
    pallas_call x1, Pallas kernels, run_adam(): pl.pallas_call(adam_kernel, grid=(steps,), out_shape=(*shapes(attn[0], Tr...  7.26 us

profile of v3, /device:TPU:0, one launch (start us, length us, event | category | flops | bytes accessed | tf_op | source)
XLA Modules:
  0.0 189.4 jit_solution(8958632310466045855)
XLA Ops:
  0.6 179.1 %shard_map.236 = (bf16[256,1024]{1,0:T(8,128)(2,1)}, f32[256,1024]{1,0:T(8,128)}, f32[13,1024]{1,0:T(8,128)}, f32[8,128]{1,0:T(8,128)}, f32[256,512]{1,0:T(8,128)}, /*index=5*/f32[1024,256]{1,0:T(8,128)}) custom-call(bf16[256,1024]{1,0:T(8,128)(2,1)} %bitcast.7, s32[1,1024]{1,0:T(1,128)} %refs_1_.2, s32[1,40]{1,0:T(1,128)} %refs_2_.2, ...), custom_call_target="tpu_custom_call" | custom-call | tf_op jit(solution)/shard_map/pallas_call | solution.py:1061
  179.7 0.0 copy-start.1
  179.8 7.3 %shard_map.237 = (f32[256,512]{1,0:T(8,128)}, f32[256,512]{1,0:T(8,128)}, f32[256,512]{1,0:T(8,128)}, bf16[256,512]{1,0:T(8,128)(2,1)}, f32[1024,256]{1,0:T(8,12...) custom-call(f32[8,128]{1,0:T(8,128)} %get-tuple-element.34.norm, ...), custom_call_target="tpu_custom_call" | custom-call | tf_op jit(solution)/shard_map/pallas_call | solution.py:1107
  187.0 0.0 copy-start
  187.0 0.0 copy-done.1
  187.0 0.8 copy.29
  187.8 0.6 copy-done
  188.4 1.0 copy.30
Async XLA Ops:
  179.7 7.3 %copy-start.1 = (bf16[256,1024]{1,0:T(8,128)(2,1)S(1)}, bf16[256,1024]{1,0:T(8,128)(2,1)}, u32[]{:S(2)}) copy-start(bf16[256,1024]{1,0:T(8,128)(2,1)} %get-tuple-element.32) | copy-start | bytes 1572868
  187.0 1.4 copy-start
